TPU v7x, 32 devices: a whole 2x2x4 slice. The times are simulated.
32 devices in a mesh: wide: 16 (over z, y, x), narrow: 2 (over core).
Axes of the slice: x: 2, y: 2, z: 4, core: 2. Of those that a mesh axis runs over, the one named last changes fastest.
Arguments:
- tokens: bfloat16 [32768, 512], P('wide', 'narrow'), may hold values from -6 to 6
- encoded: bfloat16 [32768, 512], P('wide', 'narrow'), may hold values from -6 to 6
- cotangent: bfloat16 [32768, 512], P('wide', 'narrow'), may hold values from -6 to 6
- target_lengths: int32 [256, 2], replicated, may hold values from 32 to 96, as said below
- source_segments: int32 [256, 128], replicated, may hold values from 0 to 1, as said below
- send_rows: int32 [16, 16], replicated, may hold values from 0 to 16, as said below
- proj_in: float32 [6, 512, 512], P(None, 'wide', 'narrow'), may hold values from -0.375 to 0.375
- proj_out: float32 [2, 512, 512], P(None, 'narrow', 'wide'), may hold values from -0.75 to 0.75
- ffn_in: float32 [512, 2048], P('wide', 'narrow'), may hold values from -0.25 to 0.25
- ffn_out: float32 [2048, 512], P('narrow', 'wide'), may hold values from -0.125 to 0.125
- norm_par: float32 [6, 512], P(None, 'wide')
- proj_in_moment: float32 [6, 512, 512], P(None, 'wide', 'narrow'), may hold values from -64 to 64
- proj_in_square: float32 [6, 512, 512], P(None, 'wide', 'narrow'), may hold values from 167.1168 to 668.4672
- proj_out_moment: float32 [2, 512, 512], P(None, 'narrow', 'wide'), may hold values from -64 to 64
- proj_out_square: float32 [2, 512, 512], P(None, 'narrow', 'wide'), may hold values from 167.1168 to 668.4672
- ffn_in_moment: float32 [512, 2048], P('wide', 'narrow'), may hold values from -64 to 64
- ffn_in_square: float32 [512, 2048], P('wide', 'narrow'), may hold values from 167.1168 to 668.4672
- ffn_out_moment: float32 [2048, 512], P('narrow', 'wide'), may hold values from -64 to 64
- ffn_out_square: float32 [2048, 512], P('narrow', 'wide'), may hold values from 167.1168 to 668.4672
- norm_moment: float32 [6, 512], P(None, 'wide'), may hold values from -80 to 80
- norm_square: float32 [6, 512], P(None, 'wide'), may hold values from 327.68 to 1310.72
Outputs:
- layer_out: bfloat16 [32768, 512], P('wide', 'narrow')
- tokens_grad: bfloat16 [32768, 512], P('wide', 'narrow')
- encoded_grad: bfloat16 [32768, 512], P('wide', 'narrow')
- proj_in_first: float32 [6, 512, 512], P(None, 'wide', 'narrow')
- proj_in_second: float32 [6, 512, 512], P(None, 'wide', 'narrow')
- proj_in_new: float32 [6, 512, 512], P(None, 'wide', 'narrow')
- proj_out_first: float32 [2, 512, 512], P(None, 'narrow', 'wide')
- proj_out_second: float32 [2, 512, 512], P(None, 'narrow', 'wide')
- proj_out_new: float32 [2, 512, 512], P(None, 'narrow', 'wide')
- ffn_in_first: float32 [512, 2048], P('wide', 'narrow')
- ffn_in_second: float32 [512, 2048], P('wide', 'narrow')
- ffn_in_new: float32 [512, 2048], P('wide', 'narrow')
- ffn_out_first: float32 [2048, 512], P('narrow', 'wide')
- ffn_out_second: float32 [2048, 512], P('narrow', 'wide')
- ffn_out_new: float32 [2048, 512], P('narrow', 'wide')
- norm_first: float32 [6, 512], P(None, 'wide')
- norm_second: float32 [6, 512], P(None, 'wide')
- norm_new: float32 [6, 512], P(None, 'wide')
Inputs may be any that keep to these rules, and one draw needn't show every extreme that they name: send_rows[s, d] is the row of sender s (of its 16) that goes to receiver d, or 16 where s sends d nothing. Sender s sends one row to each receiver (s + k) mod 16, for k = 0 .. 15, naming each of its rows once, so that each receiver gets exactly 16 rows. `target_lengths`: each row holds two pairs whose lengths sum to 128; some row has a pair of exactly 96 tokens. `source_segments`: pair 0 takes the first positions of a row and pair 1 the rest; each covers 128 - 96 to 96 positions, and some row has a pair of exactly 96.
All inputs are finite; a program needn't handle non-finite values.
Results may differ from a plain program's by a relative error of at most 0.02.
The roundings to bfloat16 on the way count: a program that leaves them out, or rounds other values in their place, can miss the bound.
Values may be sent and summed in bfloat16 or wider, within the bound.
No kernel may reach another device: no remote copies, remote signals or barrier semaphores. Data moves between devices by JAX's collectives and lax.ppermute only.
A program may use at most 192 MiB of HBM per device.

v0:
```python
import jax
import jax.numpy as jnp
from jax import lax
from jax.sharding import PartitionSpec as P

D = 512
H = 8
PACK = 128
STEP = 5


norm_epsilon = 1e-05
beta_first = 0.9
beta_second = 0.98
adam_epsilon = 1e-08
rate_matrix = 0.1
rate_norm = 0.5
decay_matrix = 0.01
masked_score = -1e30


def for_sending(value):

    def short(part):
        return part.astype(jnp.bfloat16) if part.dtype == jnp.float32 else part

    return jax.tree.map(short, value)


def from_behind(block, axis, distance):
    devices = range(lax.axis_size(axis))
    route = [((i - distance) % len(devices), i) for i in devices]
    return lax.ppermute(block, axis, route)


def matmul(left_side, right_side):
    return jnp.dot(left_side, right_side, preferred_element_type=jnp.float32)


def matmul_left(left_side, right_side):
    return jnp.einsum("td,te->de", left_side, right_side, preferred_element_type=jnp.float32)


def matmul_right(left_side, right_side):
    return jnp.einsum("te,de->td", left_side, right_side, preferred_element_type=jnp.float32)


def norm_forward(resid, gain, shift):
    center = resid - jnp.mean(resid, -1, keepdims=True)
    factor = lax.rsqrt(jnp.mean(center * center, -1, keepdims=True) + norm_epsilon)
    normed = center * factor
    return (normed * gain + shift, normed, factor)


def norm_backward(grad_out, normed, factor, gain):
    scaled = grad_out * gain
    grad_in = factor * (
        scaled
        - jnp.mean(scaled, -1, keepdims=True)
        - normed * jnp.mean(scaled * normed, -1, keepdims=True)
    )
    return (grad_in, jnp.sum(grad_out * normed, 0), jnp.sum(grad_out, 0))


def split_heads(values, head_count):
    return values.reshape(values.shape[0], values.shape[1], head_count, -1)


def scores_of(query_heads, key_heads, seg_query, seg_key):
    raw_scores = jnp.einsum(
        "rqhe,rkhe->rhqk", query_heads, key_heads, preferred_element_type=jnp.float32
    ) * query_heads.shape[3] ** (-0.5)
    allowed = seg_query[:, None, :, None] == seg_key[:, None, None, :]
    return jnp.where(allowed, raw_scores, masked_score)


def attend_forward(query_rows, key_rows, value_rows, seg_query, seg_key, head_count):

    def single(pieces):
        query_heads = split_heads(pieces[0], head_count)
        key_heads = split_heads(pieces[1], head_count)
        value_heads = split_heads(pieces[2], head_count)
        scores = scores_of(query_heads, key_heads, pieces[3], pieces[4])
        row_peak = jnp.max(scores, -1, keepdims=True)
        exponent = jnp.exp(scores - row_peak)
        row_total = jnp.sum(exponent, -1, keepdims=True)
        soft_probs = (exponent / row_total).astype(jnp.bfloat16)
        mixed_heads = jnp.einsum(
            "rhqk,rkhe->rqhe", soft_probs, value_heads, preferred_element_type=jnp.float32
        )
        flat_mixed = mixed_heads.reshape(mixed_heads.shape[0], mixed_heads.shape[1], -1).astype(
            jnp.bfloat16
        )
        return (flat_mixed, row_peak[..., 0] + jnp.log(row_total[..., 0]))

    return lax.map(single, (query_rows, key_rows, value_rows, seg_query, seg_key))


def attend_backward(
    query_rows, key_rows, value_rows, grad_mixed, log_total, seg_query, seg_key, head_count
):

    def single(pieces):
        query_heads = split_heads(pieces[0], head_count)
        key_heads = split_heads(pieces[1], head_count)
        value_heads = split_heads(pieces[2], head_count)
        grad_heads = split_heads(pieces[3], head_count)
        head_scale = query_heads.shape[3] ** (-0.5)
        scores = scores_of(query_heads, key_heads, pieces[5], pieces[6])
        soft_probs = jnp.exp(scores - pieces[4][..., None])
        grad_probs = jnp.einsum(
            "rqhe,rkhe->rhqk", grad_heads, value_heads, preferred_element_type=jnp.float32
        )
        grad_scores = (
            soft_probs * (grad_probs - jnp.sum(soft_probs * grad_probs, -1, keepdims=True))
        ).astype(jnp.bfloat16)
        grad_query = (
            jnp.einsum(
                "rhqk,rkhe->rqhe", grad_scores, key_heads, preferred_element_type=jnp.float32
            )
            * head_scale
        )
        grad_key = (
            jnp.einsum(
                "rhqk,rqhe->rkhe", grad_scores, query_heads, preferred_element_type=jnp.float32
            )
            * head_scale
        )
        grad_value = jnp.einsum(
            "rhqk,rqhe->rkhe",
            soft_probs.astype(jnp.bfloat16),
            grad_heads,
            preferred_element_type=jnp.float32,
        )
        row_shape = (query_heads.shape[0], query_heads.shape[1], -1)
        return (
            grad_query.reshape(row_shape).astype(jnp.bfloat16),
            grad_key.reshape(row_shape).astype(jnp.bfloat16),
            grad_value.reshape(row_shape).astype(jnp.bfloat16),
        )

    return lax.map(
        single, (query_rows, key_rows, value_rows, grad_mixed, log_total, seg_query, seg_key)
    )


def adam(weight, first_old, second_old, grad, rate, decay):
    first_new = beta_first * first_old + (1.0 - beta_first) * grad
    second_new = beta_second * second_old + (1.0 - beta_second) * grad * grad
    first_hat = first_new / (1.0 - beta_first**STEP)
    second_hat = second_new / (1.0 - beta_second**STEP)
    updated = weight - rate * (first_hat / (jnp.sqrt(second_hat) + adam_epsilon) + decay * weight)
    return (first_new, second_new, updated)


def local(
    tokens,
    encoded,
    cotangent,
    target_lengths,
    source_segments,
    send_rows,
    proj_in,
    proj_out,
    ffn_in,
    ffn_out,
    norm_par,
    proj_in_moment,
    proj_in_square,
    proj_out_moment,
    proj_out_square,
    ffn_in_moment,
    ffn_in_square,
    ffn_out_moment,
    ffn_out_square,
    norm_moment,
    norm_square,
):
    wide_count = lax.axis_size("wide")
    wide_index = lax.axis_index("wide")
    narrow_index = lax.axis_index("narrow")
    half_width = tokens.shape[1]
    rows_dev = tokens.shape[0] // PACK
    tok_count = rows_dev * PACK
    head_count = proj_in.shape[2] // (D // H)
    stride = wide_count // rows_dev
    gathered = (
        lax.all_gather(proj_in.astype(jnp.bfloat16), "wide", axis=1, tiled=True),
        lax.all_gather(proj_out.astype(jnp.bfloat16), "wide", axis=2, tiled=True),
        lax.all_gather(ffn_in.astype(jnp.bfloat16), "wide", axis=0, tiled=True),
        lax.all_gather(ffn_out.astype(jnp.bfloat16), "wide", axis=1, tiled=True),
        lax.all_gather(norm_par.astype(jnp.bfloat16), "wide", axis=1, tiled=True),
    )
    w_inputs, w_outputs, w_expand, w_reduce, norm_low = gathered
    norm_vals = norm_low.astype(jnp.float32)
    outgoing_slot = lax.dynamic_index_in_dim(send_rows, wide_index, 0, keepdims=False)
    incoming_slot = lax.dynamic_index_in_dim(send_rows, wide_index, 1, keepdims=False)
    local_ids = jnp.arange(rows_dev, dtype=jnp.int32)
    live_in = incoming_slot < rows_dev
    rank_in = jnp.cumsum(live_in.astype(jnp.int32)) - 1
    offsets = local_ids * stride
    dest_peer = (wide_index + offsets) % wide_count
    src_peer = (wide_index - offsets) % wide_count
    dest_slot = outgoing_slot[dest_peer]
    src_slot = incoming_slot[src_peer]
    arrive_pos = rank_in[src_peer]
    pos_order = jnp.sum(
        jnp.where(arrive_pos[None, :] == local_ids[:, None], local_ids[None, :], 0), 1
    )
    slot_order = jnp.sum(
        jnp.where(dest_slot[None, :] == local_ids[:, None], local_ids[None, :], 0), 1
    )

    def shaped(array):
        return array.reshape(rows_dev, PACK, -1)

    def move_out(members, mover):
        picked = tuple((member[dest_slot] for member in members))
        columns = [tuple((item[0] for item in picked))]
        for turn_index in range(1, rows_dev):
            columns.append(mover(tuple((item[turn_index] for item in picked)), turn_index * stride))
        return tuple(
            (
                jnp.stack([column[member_index] for column in columns])[pos_order]
                for member_index in range(len(members))
            )
        )

    def move_back(members, mover):
        picked = tuple((member[arrive_pos] for member in members))
        columns = [tuple((item[0] for item in picked))]
        for turn_index in range(1, rows_dev):
            columns.append(
                mover(
                    tuple((item[turn_index] for item in picked)), wide_count - turn_index * stride
                )
            )
        return tuple(
            (
                jnp.stack([column[member_index] for column in columns])[slot_order]
                for member_index in range(len(members))
            )
        )

    x_here, enc_here = move_out(
        (shaped(tokens), shaped(encoded)),
        lambda member, offset: jax.tree.map(
            lambda part, own: part.astype(own.dtype),
            from_behind(for_sending(member), "wide", offset),
            member,
        ),
    )
    grad_here = shaped(cotangent)
    row_ids = (src_peer * rows_dev + src_slot)[pos_order]
    full_rows = (
        lax.all_gather(x_here, "narrow", axis=2, tiled=True),
        lax.all_gather(enc_here, "narrow", axis=2, tiled=True),
        lax.all_gather(grad_here, "narrow", axis=2, tiled=True),
    )
    x_full = full_rows[0].reshape(tok_count, -1)
    enc_full = full_rows[1].reshape(tok_count, -1)
    grad_full = full_rows[2].reshape(tok_count, -1).astype(jnp.float32)
    lengths_here = target_lengths[row_ids]
    ends = jnp.cumsum(lengths_here, -1)
    positions = jnp.arange(PACK, dtype=jnp.int32)
    tgt_seg = jnp.sum((ends[:, None, :] <= positions[None, :, None]).astype(jnp.int32), -1).reshape(
        -1
    )
    src_seg = source_segments[row_ids].reshape(-1)
    span_rows = min(rows_dev, max(1, 512 // PACK))
    block_count = rows_dev // span_rows

    def blocked(array):
        return array.reshape((block_count, span_rows, PACK) + array.shape[1:])

    def unblocked(array):
        return array.reshape(tok_count, -1)

    def add_branch(base, partial_sum):
        return base + lax.psum(partial_sum, "narrow")

    def full_low(hidden):
        return hidden.astype(jnp.bfloat16)

    query_self = matmul(x_full, w_inputs[0]).astype(jnp.bfloat16)
    key_self = matmul(x_full, w_inputs[1]).astype(jnp.bfloat16)
    value_self = matmul(x_full, w_inputs[2]).astype(jnp.bfloat16)
    mixed_self, total_self = attend_forward(
        blocked(query_self),
        blocked(key_self),
        blocked(value_self),
        blocked(tgt_seg),
        blocked(tgt_seg),
        head_count,
    )
    mixed_self = unblocked(mixed_self)
    resid_one = add_branch(x_full.astype(jnp.float32), matmul(mixed_self, w_outputs[0]))
    hidden_one, normed_one, factor_one = norm_forward(resid_one, norm_vals[0], norm_vals[3])
    hidden_one_low = full_low(hidden_one)
    query_cross = matmul(hidden_one_low, w_inputs[3]).astype(jnp.bfloat16)
    key_cross = matmul(enc_full, w_inputs[4]).astype(jnp.bfloat16)
    value_cross = matmul(enc_full, w_inputs[5]).astype(jnp.bfloat16)
    mixed_cross, total_cross = attend_forward(
        blocked(query_cross),
        blocked(key_cross),
        blocked(value_cross),
        blocked(tgt_seg),
        blocked(src_seg),
        head_count,
    )
    mixed_cross = unblocked(mixed_cross)
    resid_two = add_branch(hidden_one, matmul(mixed_cross, w_outputs[1]))
    hidden_two, normed_two, factor_two = norm_forward(resid_two, norm_vals[1], norm_vals[4])
    hidden_two_low = full_low(hidden_two)
    pre_act = matmul(hidden_two_low, w_expand)
    act_low = jax.nn.gelu(pre_act).astype(jnp.bfloat16)
    resid_three = add_branch(hidden_two, matmul(act_low, w_reduce))
    out_rows, normed_three, factor_three = norm_forward(resid_three, norm_vals[2], norm_vals[5])
    d_resid_three, g_gain_three, g_bias_three = norm_backward(
        grad_full, normed_three, factor_three, norm_vals[2]
    )
    d_ffn = full_low(d_resid_three)
    g_reduce = matmul_left(act_low, d_ffn)
    d_act = matmul_right(d_ffn, w_reduce)
    d_pre = jax.vjp(jax.nn.gelu, pre_act)[1](d_act)[0].astype(jnp.bfloat16)
    g_expand = matmul_left(hidden_two_low, d_pre)
    d_hidden_two = add_branch(d_resid_three, matmul_right(d_pre, w_expand))
    d_resid_two, g_gain_two, g_bias_two = norm_backward(
        d_hidden_two, normed_two, factor_two, norm_vals[1]
    )
    d_cross = full_low(d_resid_two)
    g_out_cross = matmul_left(mixed_cross, d_cross)
    d_mixed_cross = matmul_right(d_cross, w_outputs[1]).astype(jnp.bfloat16)
    dq_cross, dk_cross, dv_cross = attend_backward(
        blocked(query_cross),
        blocked(key_cross),
        blocked(value_cross),
        blocked(d_mixed_cross),
        total_cross,
        blocked(tgt_seg),
        blocked(src_seg),
        head_count,
    )
    dq_cross = unblocked(dq_cross)
    dk_cross = unblocked(dk_cross)
    dv_cross = unblocked(dv_cross)
    g_query_cross = matmul_left(hidden_one_low, dq_cross)
    g_key_cross = matmul_left(enc_full, dk_cross)
    g_value_cross = matmul_left(enc_full, dv_cross)
    d_hidden_one = add_branch(d_resid_two, matmul_right(dq_cross, w_inputs[3]))
    enc_terms = matmul_right(dk_cross, w_inputs[4]) + matmul_right(dv_cross, w_inputs[5])
    enc_half = lax.psum_scatter(
        enc_terms.astype(jnp.bfloat16), "narrow", scatter_dimension=1, tiled=True
    )
    d_resid_one, g_gain_one, g_bias_one = norm_backward(
        d_hidden_one, normed_one, factor_one, norm_vals[0]
    )
    d_self = full_low(d_resid_one)
    g_out_self = matmul_left(mixed_self, d_self)
    d_mixed_self = matmul_right(d_self, w_outputs[0]).astype(jnp.bfloat16)
    dq_self, dk_self, dv_self = attend_backward(
        blocked(query_self),
        blocked(key_self),
        blocked(value_self),
        blocked(d_mixed_self),
        total_self,
        blocked(tgt_seg),
        blocked(tgt_seg),
        head_count,
    )
    dq_self = unblocked(dq_self)
    dk_self = unblocked(dk_self)
    dv_self = unblocked(dv_self)
    g_query_self = matmul_left(x_full, dq_self)
    g_key_self = matmul_left(x_full, dk_self)
    g_value_self = matmul_left(x_full, dv_self)
    d_input = add_branch(
        d_resid_one,
        matmul_right(dq_self, w_inputs[0])
        + matmul_right(dk_self, w_inputs[1])
        + matmul_right(dv_self, w_inputs[2]),
    )
    norm_grads = jnp.stack(
        [g_gain_one, g_gain_two, g_gain_three, g_bias_one, g_bias_two, g_bias_three]
    )
    half_start = narrow_index * half_width
    out_half = lax.dynamic_slice_in_dim(out_rows.astype(jnp.bfloat16), half_start, half_width, 1)
    input_half = lax.dynamic_slice_in_dim(d_input.astype(jnp.bfloat16), half_start, half_width, 1)
    local_grads = (
        jnp.stack(
            [g_query_self, g_key_self, g_value_self, g_query_cross, g_key_cross, g_value_cross]
        ),
        jnp.stack([g_out_self, g_out_cross]),
        g_expand,
        g_reduce,
        norm_grads,
    )
    summed = lax.psum(
        (local_grads[0], local_grads[1], local_grads[2], local_grads[3], local_grads[4]), "wide"
    )

    def own_share(array, axis_dim, share_width):
        return lax.dynamic_slice_in_dim(array, wide_index * share_width, share_width, axis_dim)

    shares = (
        own_share(summed[0], 1, proj_in.shape[1]),
        own_share(summed[1], 2, proj_out.shape[2]),
        own_share(summed[2], 0, ffn_in.shape[0]),
        own_share(summed[3], 1, ffn_out.shape[1]),
        own_share(summed[4], 1, norm_par.shape[1]),
    )
    upd_in = adam(proj_in, proj_in_moment, proj_in_square, shares[0], rate_matrix, decay_matrix)
    upd_out = adam(proj_out, proj_out_moment, proj_out_square, shares[1], rate_matrix, decay_matrix)
    upd_expand = adam(ffn_in, ffn_in_moment, ffn_in_square, shares[2], rate_matrix, decay_matrix)
    upd_reduce = adam(ffn_out, ffn_out_moment, ffn_out_square, shares[3], rate_matrix, decay_matrix)
    upd_norm = adam(norm_par, norm_moment, norm_square, shares[4], rate_norm, 0.0)
    back_rows = move_back(
        (shaped(input_half), shaped(enc_half)),
        lambda member, offset: jax.tree.map(
            lambda part, own: part.astype(own.dtype),
            from_behind(for_sending(member), "wide", offset),
            member,
        ),
    )
    tokens_grad = back_rows[0].reshape(tok_count, -1)
    encoded_grad = back_rows[1].reshape(tok_count, -1)
    return (
        out_half,
        tokens_grad,
        encoded_grad,
        upd_in[0],
        upd_in[1],
        upd_in[2],
        upd_out[0],
        upd_out[1],
        upd_out[2],
        upd_expand[0],
        upd_expand[1],
        upd_expand[2],
        upd_reduce[0],
        upd_reduce[1],
        upd_reduce[2],
        upd_norm[0],
        upd_norm[1],
        upd_norm[2],
    )


def solution(mesh):
    in_specs = (
        P("wide", "narrow"),
        P("wide", "narrow"),
        P("wide", "narrow"),
        P(),
        P(),
        P(),
        P(None, "wide", "narrow"),
        P(None, "narrow", "wide"),
        P("wide", "narrow"),
        P("narrow", "wide"),
        P(None, "wide"),
        P(None, "wide", "narrow"),
        P(None, "wide", "narrow"),
        P(None, "narrow", "wide"),
        P(None, "narrow", "wide"),
        P("wide", "narrow"),
        P("wide", "narrow"),
        P("narrow", "wide"),
        P("narrow", "wide"),
        P(None, "wide"),
        P(None, "wide"),
    )
    out_specs = (
        P("wide", "narrow"),
        P("wide", "narrow"),
        P("wide", "narrow"),
        P(None, "wide", "narrow"),
        P(None, "wide", "narrow"),
        P(None, "wide", "narrow"),
        P(None, "narrow", "wide"),
        P(None, "narrow", "wide"),
        P(None, "narrow", "wide"),
        P("wide", "narrow"),
        P("wide", "narrow"),
        P("wide", "narrow"),
        P("narrow", "wide"),
        P("narrow", "wide"),
        P("narrow", "wide"),
        P(None, "wide"),
        P(None, "wide"),
        P(None, "wide"),
    )
    return jax.shard_map(local, mesh=mesh, in_specs=in_specs, out_specs=out_specs, check_vma=False)
```

profile of v0, /device:TPU:0, one launch (start us, length us, event | category | flops | bytes accessed | tf_op | source)
XLA Modules:
  0.0 1029.1 jit_solution(14102758201698473752)
XLA Ops:
  10.0 7.0 collective-permute-start.14
  26.3 7.0 collective-permute-done.1
  33.2 7.4 collective-permute-done.2
  46.7 7.0 collective-permute-done.4
  53.7 7.4 collective-permute-done.5
  104.6 44.9 %all_gather.26 = bf16[2,256,512]{1,2,0:T(8,128)(2,1)} all-gather(bf16[2,256,32]{1,2,0:T(8,128)(2,1)S(1)} %convert_element_type.252), channel_id=1, replica_groups=mesh['wide'=16,'narrow'=2] {'wide'}, dimensions={2}, use_global_device_ids=true | all-gather | bytes 557056 | tf_op jit(solution)/shard_map/all_gather | solution.py:189
  149.6 8.1 collective-permute-done.16
  157.7 7.9 collective-permute-done.17
  171.8 7.3 collective-permute-done.19
  225.4 15.8 %while.54 = (s32[]{:T(128)}, bf16[4,4,128,256]{3,2,1,0:T(8,128)(2,1)}, f32[4,4,4,128]{3,2,1,0:T(4,128)S(1)}, bf16[4,4,128,256]{2,3,1,0:T(8,128)(2,1)}, s32[4,4,1...) while((s32[]{:T(128)}, ...), condition=%wide.region_7.8_spmd, body=%wide.region_4.7_spmd.sunk | while | flops 69400576 | bytes 7018609 | solution.py:96
  246.7 38.1 %all-gather.2 = bf16[16,32,6]{1,2,0:T(8,128)(2,1)S(1)} all-gather(bf16[1,32,6]{1,2,0:T(8,128)(2,1)S(1)} %convert_bitcast_fusion), channel_id=1, replica_groups=mesh['wide'=16,'narrow'=2] {'wide'}, dimensions={0}, use_global_device_ids=true | all-gather | bytes 6528 | tf_op jit(solution)/shard_map/all_gather | solution.py:192
  299.4 12.9 %while.55 = (s32[]{:T(128)}, bf16[4,4,128,256]{3,2,1,0:T(8,128)(2,1)S(1)}, f32[4,4,4,128]{3,2,1,0:T(4,128)S(1)}, bf16[4,4,128,256]{2,3,1,0:T(8,128)(2,1)}, s32[4...) while((s32[]{:T(128)}, ...), condition=%wide.region_14.15_spmd, body=%wide.region_11.14_spmd.sunk | while | flops 69400576 | bytes 7024761 | solution.py:96
  319.6 21.1 %all-reduce.11.cloned.1.call-done = f32[2048,512]{1,0:T(8,128)} async-done(((f32[2048,512]{1,0:T(8,128)}), f32[2048,512]{1,0:T(8,128)}) %all-reduce.11.cloned.1.call-update) | async-done | bytes 4194320 | tf_op jit(solution)/shard_map/psum | solution.py:280
  347.7 52.6 %all-gather.12.cloned.1.call-done = bf16[512,1024]{1,0:T(8,128)(2,1)} async-done(((bf16[32,1024]{1,0:T(8,128)(2,1)}), bf16[512,1024]{1,0:T(8,128)(2,1)}) %all-gather.12.cloned.1.call-update) | async-done | bytes 1048592 | tf_op jit(solution)/shard_map/all_gather | solution.py:190
  400.4 8.3 fusion.79
  408.7 49.2 %all-gather.14.cloned.1.call-done = bf16[1024,512]{0,1:T(8,128)(2,1)} async-done(((bf16[1024,32]{0,1:T(8,128)(2,1)}), bf16[1024,512]{0,1:T(8,128)(2,1)}) %all-gather.14.cloned.1.call-update) | async-done | bytes 1048592 | tf_op jit(solution)/shard_map/all_gather | solution.py:191
  457.8 8.7 fusion.81
  471.6 29.0 %all-reduce.13.cloned.1.call-done = f32[2048,512]{1,0:T(8,128)} async-done(((f32[2048,512]{1,0:T(8,128)}), f32[2048,512]{1,0:T(8,128)}) %all-reduce.13.cloned.1.call-update) | async-done | bytes 4194320 | tf_op jit(solution)/shard_map/psum | solution.py:280
  513.0 7.1 fusion.25
  526.8 29.5 %all-reduce.15.cloned.1.call-done = f32[2048,512]{1,0:T(8,128)} async-done(((f32[2048,512]{1,0:T(8,128)}), f32[2048,512]{1,0:T(8,128)}) %all-reduce.15.cloned.1.call-update) | async-done | bytes 4194320 | tf_op jit(solution)/shard_map/psum | solution.py:280
  569.0 33.6 %while.56 = (s32[]{:T(128)}, bf16[4,4,128,256]{3,2,1,0:T(8,128)(2,1)}, bf16[4,4,128,256]{3,2,1,0:T(8,128)(2,1)S(1)}, bf16[4,4,128,256]{3,2,1,0:T(8,128)(2,1)}, b...) while((s32[]{:T(128)}, ...), condition=%wide.region_28.29_spmd, body=%wide.region_26.28_spmd.sunk | while | flops 170850304 | bytes 16437409 | solution.py:142
  613.0 23.8 %all-reduce.17.cloned.1.call-done = f32[2048,512]{1,0:T(8,128)} async-done(((f32[2048,512]{1,0:T(8,128)}), f32[2048,512]{1,0:T(8,128)}) %all-reduce.17.cloned.1.call-update) | async-done | bytes 4194320 | tf_op jit(solution)/shard_map/psum | solution.py:280
  649.2 36.4 %while.57 = (s32[]{:T(128)}, bf16[4,4,128,256]{3,2,1,0:T(8,128)(2,1)}, bf16[4,4,128,256]{3,2,1,0:T(8,128)(2,1)S(1)}, bf16[4,4,128,256]{3,2,1,0:T(8,128)(2,1)}, b...) while((s32[]{:T(128)}, ...), condition=%wide.region_34.35_spmd, body=%wide.region_32.34_spmd.sunk | while | flops 170850304 | bytes 16431253 | solution.py:142
  693.1 7.4 fusion.77
  700.6 9.3 fusion.50
  739.8 77.4 %psum.87 = f32[6,512]{1,0:T(8,128)S(1)} all-reduce(f32[6,512]{1,0:T(8,128)S(1)} %stack.323), channel_id=1, replica_groups=mesh['wide'=16,'narrow'=2] {'wide'}, use_global_device_ids=true, to_apply=%region_48.49 | all-reduce | flops 3072 | bytes 24576 | tf_op jit(solution)/shard_map/psum | solution.py:398
  881.0 9.8 collective-permute-done.55
  939.9 7.8 collective-permute-start.36
  947.7 7.1 collective-permute-done.36
  954.9 9.1 collective-permute-done.37
  984.8 9.9 collective-permute-done.40
  996.4 18.9 %all-reduce.21.cloned.1.call-done = (f32[6,512,256]{2,1,0:T(8,128)}, f32[2,256,512]{1,2,0:T(8,128)}, f32[512,1024]{1,0:T(8,128)}, f32[1024,512]{0,1:T(8,128)}) async-done(((f32[6,512,256]{2,1,0:T(8,128)}, f32[2,256,512]{1,2,0:T(8,128)}, f32[512,1024]{1,0:T(8,128)}, f32[1024,512]{0,1:T(8,128)}), (f32[6,512,256]{2,1,0:T(8,128)}, f32[2,256,512]{1,2,0:T(8,128)}, f32[512,1024]{1,0:T(8,128)}, ...) | async-done | bytes 8388624 | tf_op jit(solution)/shard_map/psum | solution.py:398
  (700 shorter events, 484.4 us)
Async XLA Ops:
  7.2 207.3 %all-gather.18.cloned.1.call-start = ((), (), s32[]{:S(2)}) async-start(), calls=%async_computation.12 | async-start | bytes 3145728 | tf_op jit(solution)/shard_map/all_gather | solution.py:256
  10.0 78.9 %collective-permute-start.14 = (bf16[128,256]{1,0:T(8,128)(2,1)S(1)}, bf16[128,256]{1,0:T(8,128)(2,1)S(1)}, u32[]{:S(2)}, u32[]{:S(2)}) collective-permute-start(bf16[128,256]{1,0:T(8,128)(2,1)S(1)} %get-tuple-element.682), channel_id=1, source_target_pairs={{2,0},{4,2},{6,4},{8,6},{10,8},{12,10},{14,12},{16,14},{18,16},{20... | collective-permute-start | bytes 196616 | tf_op jit(solution)/shard_map/ppermute | solution.py:33
  17.0 71.9 %collective-permute-start.13 = (bf16[128,256]{1,0:T(8,128)(2,1)S(1)}, bf16[128,256]{1,0:T(8,128)(2,1)S(1)}, u32[]{:S(2)}, u32[]{:S(2)}) collective-permute-start(bf16[128,256]{1,0:T(8,128)(2,1)S(1)} %get-tuple-element.683), channel_id=1, source_target_pairs={{4,0},{6,2},{8,4},{10,6},{12,8},{14,10},{16,12},{18,14},{20,16},{2... | collective-permute-start | bytes 196616 | tf_op jit(solution)/shard_map/ppermute | solution.py:33
  17.5 71.4 %collective-permute-start.12 = (bf16[128,256]{1,0:T(8,128)(2,1)S(1)}, bf16[128,256]{1,0:T(8,128)(2,1)S(1)}, u32[]{:S(2)}, u32[]{:S(2)}) collective-permute-start(bf16[128,256]{1,0:T(8,128)(2,1)S(1)} %get-tuple-element.684), channel_id=1, source_target_pairs={{6,0},{8,2},{10,4},{12,6},{14,8},{16,10},{18,12},{20,14},{22,16},{... | collective-permute-start | bytes 196616 | tf_op jit(solution)/shard_map/ppermute | solution.py:33
  17.9 70.9 %collective-permute-start.11 = (bf16[128,256]{1,0:T(8,128)(2,1)S(1)}, bf16[128,256]{1,0:T(8,128)(2,1)S(1)}, u32[]{:S(2)}, u32[]{:S(2)}) collective-permute-start(bf16[128,256]{1,0:T(8,128)(2,1)S(1)} %get-tuple-element.685), channel_id=1, source_target_pairs={{8,0},{10,2},{12,4},{14,6},{16,8},{18,10},{20,12},{22,14},{24,16},... | collective-permute-start | bytes 196616 | tf_op jit(solution)/shard_map/ppermute | solution.py:33
  90.5 124.1 %all-gather.10.cloned.1.call-start = ((), (), s32[]{:S(2)}) async-start(), calls=%async_computation.1 | async-start | bytes 1671168 | tf_op jit(solution)/shard_map/all_gather | solution.py:188
  92.5 120.3 %collective-permute-start.29 = (bf16[128,256]{1,0:T(8,128)(2,1)S(1)}, bf16[128,256]{1,0:T(8,128)(2,1)S(1)}, u32[]{:S(2)}, u32[]{:S(2)}) collective-permute-start(bf16[128,256]{1,0:T(8,128)(2,1)S(1)} %get-tuple-element.698), channel_id=1, source_target_pairs={{2,0},{4,2},{6,4},{8,6},{10,8},{12,10},{14,12},{16,14},{18,16},{20... | collective-permute-start | bytes 196616 | tf_op jit(solution)/shard_map/ppermute | solution.py:33
  97.8 115.1 %collective-permute-start.28 = (bf16[128,256]{1,0:T(8,128)(2,1)S(1)}, bf16[128,256]{1,0:T(8,128)(2,1)S(1)}, u32[]{:S(2)}, u32[]{:S(2)}) collective-permute-start(bf16[128,256]{1,0:T(8,128)(2,1)S(1)} %get-tuple-element.699), channel_id=1, source_target_pairs={{4,0},{6,2},{8,4},{10,6},{12,8},{14,10},{16,12},{18,14},{20,16},{2... | collective-permute-start | bytes 196616 | tf_op jit(solution)/shard_map/ppermute | solution.py:33
  97.8 115.0 %collective-permute-start.27 = (bf16[128,256]{1,0:T(8,128)(2,1)S(1)}, bf16[128,256]{1,0:T(8,128)(2,1)S(1)}, u32[]{:S(2)}, u32[]{:S(2)}) collective-permute-start(bf16[128,256]{1,0:T(8,128)(2,1)S(1)} %get-tuple-element.700), channel_id=1, source_target_pairs={{6,0},{8,2},{10,4},{12,6},{14,8},{16,10},{18,12},{20,14},{22,16},{... | collective-permute-start | bytes 196616 | tf_op jit(solution)/shard_map/ppermute | solution.py:33
  98.7 114.0 %collective-permute-start.26 = (bf16[128,256]{1,0:T(8,128)(2,1)S(1)}, bf16[128,256]{1,0:T(8,128)(2,1)S(1)}, u32[]{:S(2)}, u32[]{:S(2)}) collective-permute-start(bf16[128,256]{1,0:T(8,128)(2,1)S(1)} %get-tuple-element.701), channel_id=1, source_target_pairs={{8,0},{10,2},{12,4},{14,6},{16,8},{18,10},{20,12},{22,14},{24,16},... | collective-permute-start | bytes 196616 | tf_op jit(solution)/shard_map/ppermute | solution.py:33
  98.7 50.8 %collective-permute-start.15 = (bf16[128,256]{1,0:T(8,128)(2,1)S(1)}, bf16[128,256]{1,0:T(8,128)(2,1)S(1)}, u32[]{:S(2)}, u32[]{:S(2)}) collective-permute-start(bf16[128,256]{1,0:T(8,128)(2,1)S(1)} %get-tuple-element.712), channel_id=1, source_target_pairs={{30,0},{0,2},{2,4},{4,6},{6,8},{8,10},{10,12},{12,14},{14,16},{16,... | collective-permute-start | bytes 196616 | tf_op jit(solution)/shard_map/ppermute | solution.py:33
  102.2 182.8 %all-gather.20.cloned.1.call-start = ((), (), s32[]{:S(2)}) async-start(), calls=%async_computation.13 | async-start | bytes 3145728 | tf_op jit(solution)/shard_map/all_gather | solution.py:257
  214.5 77.7 %all-reduce.9.cloned.1.call-start = ((), (), s32[]{:S(2)}) async-start(), calls=%async_computation.2 | async-start | bytes 8388608 | tf_op jit(solution)/shard_map/psum | solution.py:280
  245.2 95.5 %all-reduce.11.cloned.1.call-start = ((), (), s32[]{:S(2)}) async-start(), calls=%async_computation.3 | async-start | bytes 8388608 | tf_op jit(solution)/shard_map/psum | solution.py:280
  316.2 84.1 %all-gather.12.cloned.1.call-start = ((), (), s32[]{:S(2)}) async-start(), calls=%async_computation.4 | async-start | bytes 1114112 | tf_op jit(solution)/shard_map/all_gather | solution.py:190
  317.8 140.0 %all-gather.14.cloned.1.call-start = ((), (), s32[]{:S(2)}) async-start(), calls=%async_computation.5 | async-start | bytes 1114112 | tf_op jit(solution)/shard_map/all_gather | solution.py:191
  318.5 150.0 %all-gather.16.cloned.1.call-start = ((), (), s32[]{:S(2)}) async-start(), calls=%async_computation.7 | async-start | bytes 3145728 | tf_op jit(solution)/shard_map/all_gather | solution.py:258
  319.3 181.4 %all-reduce.13.cloned.1.call-start = ((), (), s32[]{:S(2)}) async-start(), calls=%async_computation.6 | async-start | bytes 8388608 | tf_op jit(solution)/shard_map/psum | solution.py:280
  466.5 89.8 %all-reduce.15.cloned.1.call-start = ((), (), s32[]{:S(2)}) async-start(), calls=%async_computation.8 | async-start | bytes 8388608 | tf_op jit(solution)/shard_map/psum | solution.py:280
  526.6 110.2 %all-reduce.17.cloned.1.call-start = ((), (), s32[]{:S(2)}) async-start(), calls=%async_computation.9 | async-start | bytes 8388608 | tf_op jit(solution)/shard_map/psum | solution.py:280
  607.0 119.9 %reduce-scatter.2.cloned.1.call-start = ((), (), s32[]{:S(2)}) async-start(), calls=%async_computation.11 | async-start | bytes 3145728 | tf_op jit(solution)/shard_map/reduce_scatter | solution.py:352
  612.7 278.3 %all-reduce.19.cloned.1.call-start = ((), (), s32[]{:S(2)}) async-start(), calls=%async_computation.10 | async-start | bytes 8388608 | tf_op jit(solution)/shard_map/psum | solution.py:280
  692.8 322.4 %all-reduce.21.cloned.1.call-start = ((), (), s32[]{:S(2)}) async-start(), calls=%async_computation.14 | async-start | bytes 16777216 | tf_op jit(solution)/shard_map/psum | solution.py:398
  729.4 168.7 %collective-permute-start.59 = (bf16[128,256]{1,0:T(8,128)(2,1)}, bf16[128,256]{1,0:T(8,128)(2,1)}, u32[]{:S(2)}, u32[]{:S(2)}) collective-permute-start(bf16[128,256]{1,0:T(8,128)(2,1)} %get-tuple-element.650), channel_id=1, source_target_pairs={{30,0},{0,2},{2,4},{4,6},{6,8},{8,10},{10,12},{12,14},{14,16},{16,... | collective-permute-start | bytes 196616 | tf_op jit(solution)/shard_map/ppermute | solution.py:33
  731.2 159.8 %collective-permute-start.58 = (bf16[128,256]{1,0:T(8,128)(2,1)S(1)}, bf16[128,256]{1,0:T(8,128)(2,1)S(1)}, u32[]{:S(2)}, u32[]{:S(2)}) collective-permute-start(bf16[128,256]{1,0:T(8,128)(2,1)S(1)} %get-tuple-element.651), channel_id=1, source_target_pairs={{28,0},{30,2},{0,4},{2,6},{4,8},{6,10},{8,12},{10,14},{12,16},{14,... | collective-permute-start | bytes 196616 | tf_op jit(solution)/shard_map/ppermute | solution.py:33
  732.6 158.3 %collective-permute-start.57 = (bf16[128,256]{1,0:T(8,128)(2,1)S(1)}, bf16[128,256]{1,0:T(8,128)(2,1)S(1)}, u32[]{:S(2)}, u32[]{:S(2)}) collective-permute-start(bf16[128,256]{1,0:T(8,128)(2,1)S(1)} %get-tuple-element.652), channel_id=1, source_target_pairs={{26,0},{28,2},{30,4},{0,6},{2,8},{4,10},{6,12},{8,14},{10,16},{12,... | collective-permute-start | bytes 196616 | tf_op jit(solution)/shard_map/ppermute | solution.py:33
  735.0 155.9 %collective-permute-start.56 = (bf16[128,256]{1,0:T(8,128)(2,1)S(1)}, bf16[128,256]{1,0:T(8,128)(2,1)S(1)}, u32[]{:S(2)}, u32[]{:S(2)}) collective-permute-start(bf16[128,256]{1,0:T(8,128)(2,1)S(1)} %get-tuple-element.653), channel_id=1, source_target_pairs={{24,0},{26,2},{28,4},{30,6},{0,8},{2,10},{4,12},{6,14},{8,16},{10,... | collective-permute-start | bytes 196616 | tf_op jit(solution)/shard_map/ppermute | solution.py:33
  736.5 81.4 %collective-permute-start.45 = (bf16[128,256]{1,0:T(8,128)(2,1)S(1)}, bf16[128,256]{1,0:T(8,128)(2,1)S(1)}, u32[]{:S(2)}, u32[]{:S(2)}) collective-permute-start(bf16[128,256]{1,0:T(8,128)(2,1)S(1)} %get-tuple-element.664), channel_id=1, source_target_pairs={{2,0},{4,2},{6,4},{8,6},{10,8},{12,10},{14,12},{16,14},{18,16},{20... | collective-permute-start | bytes 196616 | tf_op jit(solution)/shard_map/ppermute | solution.py:33
  900.6 94.2 %collective-permute-start.44 = (bf16[128,256]{1,0:T(8,128)(2,1)}, bf16[128,256]{1,0:T(8,128)(2,1)S(1)}, u32[]{:S(2)}, u32[]{:S(2)}) collective-permute-start(bf16[128,256]{1,0:T(8,128)(2,1)} %get-tuple-element.666), channel_id=1, source_target_pairs={{30,0},{0,2},{2,4},{4,6},{6,8},{8,10},{10,12},{12,14},{14,16},{16,... | collective-permute-start | bytes 196616 | tf_op jit(solution)/shard_map/ppermute | solution.py:33
  900.6 94.1 %collective-permute-start.43 = (bf16[128,256]{1,0:T(8,128)(2,1)}, bf16[128,256]{1,0:T(8,128)(2,1)S(1)}, u32[]{:S(2)}, u32[]{:S(2)}) collective-permute-start(bf16[128,256]{1,0:T(8,128)(2,1)} %get-tuple-element.667), channel_id=1, source_target_pairs={{28,0},{30,2},{0,4},{2,6},{4,8},{6,10},{8,12},{10,14},{12,16},{14,... | collective-permute-start | bytes 196616 | tf_op jit(solution)/shard_map/ppermute | solution.py:33
  902.5 92.3 %collective-permute-start.42 = (bf16[128,256]{1,0:T(8,128)(2,1)}, bf16[128,256]{1,0:T(8,128)(2,1)S(1)}, u32[]{:S(2)}, u32[]{:S(2)}) collective-permute-start(bf16[128,256]{1,0:T(8,128)(2,1)} %get-tuple-element.668), channel_id=1, source_target_pairs={{26,0},{28,2},{30,4},{0,6},{2,8},{4,10},{6,12},{8,14},{10,16},{12,... | collective-permute-start | bytes 196616 | tf_op jit(solution)/shard_map/ppermute | solution.py:33
  905.7 89.0 %collective-permute-start.41 = (bf16[128,256]{1,0:T(8,128)(2,1)}, bf16[128,256]{1,0:T(8,128)(2,1)S(1)}, u32[]{:S(2)}, u32[]{:S(2)}) collective-permute-start(bf16[128,256]{1,0:T(8,128)(2,1)} %get-tuple-element.669), channel_id=1, source_target_pairs={{24,0},{26,2},{28,4},{30,6},{0,8},{2,10},{4,12},{6,14},{8,16},{10,... | collective-permute-start | bytes 196616 | tf_op jit(solution)/shard_map/ppermute | solution.py:33
  (107 other events, 2224.9 us)
Sparse Core Ops, SparseCore 0:
  90.7 11.2 all-gather.17
  105.3 60.8 all-gather.9
  214.6 10.6 all-gather.19
  245.4 28.7 all-reduce.8
  316.4 24.3 all-reduce.10
  343.9 56.4 all-gather.11
  403.7 54.0 all-gather.13
  459.3 9.1 all-gather.15
  471.0 29.6 all-reduce.12
  526.7 29.5 all-reduce.14
  607.1 29.6 all-reduce.16
  638.9 10.7 reduce-scatter.1
  693.0 29.6 all-reduce.18
  730.0 285.1 all-reduce.20
where the time goes:
time: 1040 us; the launch traced here: 1030 us
  waiting for transfers between devices  449 us (43%)
  blocking collectives  160 us (15%)
  matrix products  119 us (11%)
  local copies, waits for them, and re-layouts  117 us (11%)
  starting transfers between devices  109 us (10%)
  other arithmetic  58.4 us (6%)
  between operations  15.7 us (2%)
    ppermute x60, waiting for transfers between devices, from_behind(): return lax.ppermute(block, axis, route)  222 us
    ppermute x60, starting transfers between devices, from_behind(): return lax.ppermute(block, axis, route)  107 us
    psum x6, waiting for transfers between devices, add_branch(): return base + lax.psum(partial_sum, 'narrow')  104 us
    psum x1, blocking collectives, local(): lax.psum((local_grads[0], local_grads[1], local_grads[2], local_grads[3],...  77.4 us
    all_gather x1, waiting for transfers between devices, local(): lax.all_gather(ffn_in.astype(jnp.bfloat16), 'wide', axis=0, tiled=True)  52.6 us
    all_gather x1, waiting for transfers between devices, local(): lax.all_gather(ffn_out.astype(jnp.bfloat16), 'wide', axis=1, tiled=True)  49.2 us
    dynamic_slice x56, local copies, waits for them, and re-layouts, attend_forward(): lax.map(single, (query_rows, key_rows, value_rows, seg_query, seg_key))  48.6 us
    all_gather x1, blocking collectives, local(): lax.all_gather(proj_out.astype(jnp.bfloat16), 'wide', axis=2, tiled=True)  44.9 us
  transfers between devices with their start and end apart: 74, of which 49 were waited for; matrix products, arithmetic and copies ran while one was open for 17% of the time, Pallas kernels for 0%

commit v1 on v0

v1 whole, which is shorter than its diff:
```python
import functools
import math

import jax
import jax.numpy as jnp
from jax import lax
from jax.experimental import pallas as pl
from jax.experimental.pallas import tpu as pltpu
from jax.sharding import PartitionSpec as P

D = 512
H = 8
HD = D // H
PACK = 128
STEP = 5
CH = 32
HALF = D // 2
PIECES = D // CH
SLOTS = 8
TOK = SLOTS * PACK
BLK = 256
GRID = TOK // BLK
PER = BLK // PACK

norm_epsilon = 1e-05
beta_first = 0.9
beta_second = 0.98
adam_epsilon = 1e-08
rate_matrix = 0.1
rate_norm = 0.5
decay_matrix = 0.01
masked_score = -1e30

CORE = 0
PIECE = 1
ROW = PIECE + PIECES
FIRST = ROW + 2 * SLOTS
SECOND = FIRST + SLOTS
GLOBAL = SECOND + SLOTS

BF = jnp.bfloat16
F32 = jnp.float32


def dot(a, b):
    return jnp.dot(a, b, preferred_element_type=F32)


def dot_nt(a, b):
    return lax.dot_general(a, b, (((1,), (1,)), ((), ())), preferred_element_type=F32)


def dot_tn(a, b):
    return lax.dot_general(a, b, (((0,), (0,)), ((), ())), preferred_element_type=F32)


def sds(shape, dtype=BF):
    return jax.ShapeDtypeStruct(shape, dtype)


def call(body, grid, in_specs, out_specs, out_shape, scratch=(), flops=0, nbytes=0, prefetch=1):
    return pl.pallas_call(
        body,
        grid_spec=pltpu.PrefetchScalarGridSpec(
            num_scalar_prefetch=prefetch,
            grid=grid,
            in_specs=in_specs,
            out_specs=out_specs,
            scratch_shapes=list(scratch),
        ),
        out_shape=out_shape,
        cost_estimate=pl.CostEstimate(flops=flops, bytes_accessed=nbytes, transcendentals=0),
        compiler_params=pltpu.CompilerParams(
            vmem_limit_bytes=56 * 1024 * 1024, dimension_semantics=("arbitrary",) * len(grid)
        ),
    )


ANY = pl.BlockSpec(memory_space=pl.ANY)


def rows_spec(width, rows=BLK):
    return pl.BlockSpec((rows, width), lambda i, meta: (i, 0))


def fixed_spec(shape):
    return pl.BlockSpec(shape, lambda i, meta: (0,) * len(shape))


def slot_spec(k):
    return pl.BlockSpec((PACK, HALF), lambda i, meta: (meta[ROW + PER * i + k], 0))


def pack_body(pin, pout, win, wout, norm, g0, g1, g2):
    eye = (
        lax.broadcasted_iota(jnp.int32, (CH, CH), 0) == lax.broadcasted_iota(jnp.int32, (CH, CH), 1)
    ).astype(BF)
    wide = (
        lax.broadcasted_iota(jnp.int32, (CH, HALF), 1) % CH
        == lax.broadcasted_iota(jnp.int32, (CH, HALF), 0)
    ).astype(BF)
    place = (
        lax.broadcasted_iota(jnp.int32, (CH, 6), 0) == lax.broadcasted_iota(jnp.int32, (CH, 6), 1)
    ).astype(BF)
    for m in range(3):
        g0[m] = pin[m].astype(BF)
        g1[1 + m] = pin[3 + m].astype(BF)
    g1[0] = dot_nt(eye, pout[0].astype(BF)).astype(BF)
    g1[4] = dot(dot(place, norm[...].astype(BF)).astype(BF), wide).astype(BF)
    g2[0] = dot_nt(eye, pout[1].astype(BF)).astype(BF)
    blocks = win.shape[1] // HALF
    for b in range(blocks):
        g2[1 + b] = win[:, b * HALF : (b + 1) * HALF].astype(BF)
        g2[1 + blocks + b] = dot_nt(eye, wout[b * HALF : (b + 1) * HALF, :].astype(BF)).astype(BF)


def pack(pin, pout, win, wout, norm):
    blocks = win.shape[1] // HALF
    counts = (3, 5, 1 + 2 * blocks)
    return pl.pallas_call(
        pack_body,
        out_shape=tuple(sds((c, CH, HALF)) for c in counts),
        compiler_params=pltpu.CompilerParams(vmem_limit_bytes=56 * 1024 * 1024),
        cost_estimate=pl.CostEstimate(flops=10**6, bytes_accessed=6 * 10**6, transcendentals=0),
    )(pin, pout, win, wout, norm)


def load_weights(meta, pieces, w_ref, sems):
    copies = []
    for a, piece in enumerate(pieces):
        half, group = divmod(a, len(pieces) // 2)
        per = piece.shape[0]
        for j in range(per):
            row = pl.multiple_of(meta[PIECE + group * per + j] * CH, CH)
            copies.append(
                pltpu.make_async_copy(
                    piece.at[j],
                    w_ref.at[:, pl.ds(row, CH), pl.ds(half * HALF, HALF)],
                    sems.at[a],
                )
            )
    for c in copies:
        c.start()
    return copies


def lane_masks():
    low = lax.broadcasted_iota(jnp.int32, (1, PACK), 1) < HD
    return low.astype(F32).astype(BF), (1.0 - low.astype(F32)).astype(BF)


def low_lanes():
    return lax.broadcasted_iota(jnp.int32, (PACK, PACK), 1) < HD


def pair_forward(q, k, v, mask2, low, high, pick):
    scale = HD**-0.5
    qs = jnp.concatenate([q * (low * scale), q * (high * scale)], 0)
    s = jnp.where(mask2, dot_nt(qs, k), masked_score)
    e = jnp.exp(s - jnp.max(s, -1, keepdims=True))
    p = (e * (1.0 / jnp.sum(e, -1, keepdims=True))).astype(BF)
    r = dot(p, v)
    return p, jnp.where(pick, r[:PACK], r[PACK:]).astype(BF)


def pair_backward(q, k, v, p, dm, low, high, pick):
    scale = HD**-0.5
    qs = jnp.concatenate([q * (low * scale), q * (high * scale)], 0)
    dms = jnp.concatenate([dm * low, dm * high], 0)
    dp = dot_nt(dms, v)
    pf = p.astype(F32)
    ds = (pf * (dp - jnp.sum(pf * dp, -1, keepdims=True))).astype(BF)
    r = dot(ds, k)
    dq = (jnp.where(pick, r[:PACK], r[PACK:]) * scale).astype(BF)
    return dq, dot_tn(ds, qs).astype(BF), dot_tn(p, dms).astype(BF)


def norm_forward(r):
    center = r - jnp.mean(r, -1, keepdims=True)
    rstd = lax.rsqrt(jnp.mean(center * center, -1, keepdims=True) + norm_epsilon)
    return center * rstd, rstd


def norm_backward(dy, n, rstd, gain):
    dn = dy * gain
    dr = rstd * (dn - jnp.mean(dn, -1, keepdims=True) - n * jnp.mean(dn * n, -1, keepdims=True))
    return dr, jnp.sum(dy * n, 0, keepdims=True), jnp.sum(dy, 0, keepdims=True)


def segments(meta, slot, dim):
    at = lax.broadcasted_iota(jnp.int32, (PACK, PACK), dim)
    one = (at >= meta[FIRST + slot]).astype(jnp.int32)
    return one + (at >= meta[SECOND + slot]).astype(jnp.int32)


def natural(meta, own, other):
    first = meta[CORE] == 0
    return jnp.concatenate([jnp.where(first, own, other), jnp.where(first, other, own)], 1)


def halves(meta, full):
    first = meta[CORE] == 0
    lo, hi = full[:, :HALF], full[:, HALF:]
    return jnp.where(first, lo, hi), jnp.where(first, hi, lo)


def self_forward_body(*refs):
    meta, own0, oth0, own1, oth1 = refs[:5]
    pieces = refs[5:13]
    x_ref, q_ref, k_ref, v_ref, m_ref, p_ref, w_ref, sems = refs[13:]
    i = pl.program_id(0)

    @pl.when(i == 0)
    def _():
        for c in load_weights(meta, pieces, w_ref, sems):
            c.wait()

    x = jnp.concatenate(
        [natural(meta, own0[...], oth0[...]), natural(meta, own1[...], oth1[...])], 0
    )
    x_ref[...] = x
    q_ref[...] = dot(x, w_ref[0]).astype(BF)
    k_ref[...] = dot(x, w_ref[1]).astype(BF)
    v_ref[...] = dot(x, w_ref[2]).astype(BF)
    low, high = lane_masks()
    pick = low_lanes()
    for s in range(PER):
        slot = PER * i + s
        mask = segments(meta, slot, 0) == segments(meta, slot, 1)
        mask2 = jnp.concatenate([mask, mask], 0)
        rows = slice(s * PACK, (s + 1) * PACK)
        for h in range(H // 2):
            cols = slice(h * PACK, (h + 1) * PACK)
            p, m = pair_forward(
                q_ref[rows, cols], k_ref[rows, cols], v_ref[rows, cols], mask2, low, high, pick
            )
            p_ref[s * (H // 2) + h] = p
            m_ref[rows, cols] = m


def self_forward(meta, tok_own, tok_oth, pieces):
    full = rows_spec(D)
    p_spec = pl.BlockSpec((PER * H // 2, 2 * PACK, PACK), lambda i, meta: (i, 0, 0))
    return call(
        self_forward_body,
        (GRID,),
        [slot_spec(0), slot_spec(0), slot_spec(1), slot_spec(1)] + [ANY] * 8,
        (full, full, full, full, full, p_spec, fixed_spec((3, D, D))),
        (
            (sds((TOK, D)),) * 5
            + (sds((SLOTS * H // 2, 2 * PACK, PACK)), sds((3, D, D)))
        ),
        [pltpu.SemaphoreType.DMA((8,))],
        flops=2 * TOK * D * D * 4,
        nbytes=10 * 2**20,
    )(meta, tok_own, tok_oth, tok_own, tok_oth, *pieces)


def cross_forward_body(*refs):
    meta, x_ref, m_in, own0, oth0, own1, oth1, seg0, seg1 = refs[:9]
    pieces = refs[9:17]
    (n_ref, r_ref, h_ref, e_ref, q_ref, k_ref, v_ref, m_ref, p_ref, w_ref, norm_ref, sems) = refs[17:]
    i = pl.program_id(0)

    @pl.when(i == 0)
    def _():
        for c in load_weights(meta, pieces, w_ref, sems):
            c.wait()
        lane = lax.broadcasted_iota(jnp.int32, (8, HALF), 1) // CH
        for half in range(2):
            total = jnp.zeros((8, HALF), F32)
            for j in range(PIECES // 2):
                at = (half * (PIECES // 2) + j) * CH
                part = w_ref[4, at : at + 16, :HALF][:8].astype(F32)
                total = total + jnp.where(lane == j, part, 0.0)
            norm_ref[:, half * HALF : (half + 1) * HALF] = total

    n, rstd = norm_forward(x_ref[...].astype(F32) + dot_nt(m_in[...], w_ref[0]))
    n_ref[...] = n
    r_ref[...] = jnp.broadcast_to(rstd, (BLK, PACK))
    h = (n * norm_ref[0:1, :] + norm_ref[3:4, :]).astype(BF)
    h_ref[...] = h
    enc = jnp.concatenate(
        [natural(meta, own0[...], oth0[...]), natural(meta, own1[...], oth1[...])], 0
    )
    e_ref[...] = enc
    q_ref[...] = dot(h, w_ref[1]).astype(BF)
    k_ref[...] = dot(enc, w_ref[2]).astype(BF)
    v_ref[...] = dot(enc, w_ref[3]).astype(BF)
    low, high = lane_masks()
    pick = low_lanes()
    for s, seg in enumerate((seg0, seg1)):
        mask = segments(meta, PER * i + s, 0) == seg[0]
        mask2 = jnp.concatenate([mask, mask], 0)
        rows = slice(s * PACK, (s + 1) * PACK)
        for h_at in range(H // 2):
            cols = slice(h_at * PACK, (h_at + 1) * PACK)
            p, m = pair_forward(
                q_ref[rows, cols], k_ref[rows, cols], v_ref[rows, cols], mask2, low, high, pick
            )
            p_ref[s * (H // 2) + h_at] = p
            m_ref[rows, cols] = m


def cross_forward(meta, x, m, enc_own, enc_oth, segs, pieces):
    full = rows_spec(D)
    p_spec = pl.BlockSpec((PER * H // 2, 2 * PACK, PACK), lambda i, meta: (i, 0, 0))

    def seg_spec(k):
        return pl.BlockSpec((1, 1, PACK), lambda i, meta: (meta[GLOBAL + PER * i + k], 0, 0))

    return call(
        cross_forward_body,
        (GRID,),
        [full, full, slot_spec(0), slot_spec(0), slot_spec(1), slot_spec(1), seg_spec(0), seg_spec(1)]
        + [ANY] * 8,
        (full, rows_spec(PACK), full, full, full, full, full, full, p_spec)
        + (fixed_spec((5, D, D)), fixed_spec((8, D))),
        (sds((TOK, D), F32), sds((TOK, PACK), F32))
        + (sds((TOK, D)),) * 6
        + (sds((SLOTS * H // 2, 2 * PACK, PACK)), sds((5, D, D)), sds((8, D), F32)),
        [pltpu.SemaphoreType.DMA((8,))],
        flops=2 * TOK * D * D * 5,
        nbytes=16 * 2**20,
    )(meta, x, m, enc_own, enc_oth, enc_own, enc_oth, segs, segs, *pieces)


def gelu_both(v):
    c = math.sqrt(2.0 / math.pi)
    v2 = v * v
    t = jnp.tanh(c * (v + 0.044715 * (v * v2)))
    cdf = 0.5 + 0.5 * t
    return v * cdf, cdf + (0.5 * v) * (1.0 - t * t) * (c + (3.0 * 0.044715 * c) * v2)


def ffn_body(*refs):
    meta, n_in, m_in, norm, cot_own, cot_oth = refs[:6]
    pieces = refs[6:14]
    out_own, out_oth, dr_ref, po_ref, g_own, g_oth, ng_ref = refs[14:21]
    w_ref, act_ref, pre_ref, slope_ref, df_t, h_t, sems = refs[21:]
    i = pl.program_id(0)
    blocks = (w_ref.shape[0] - 1) // 2

    @pl.when(i == 0)
    def _():
        for c in load_weights(meta, pieces, w_ref, sems):
            c.wait()
        po_ref[...] = w_ref[0]
        ng_ref[...] = jnp.zeros_like(ng_ref)

    at = pl.multiple_of(i * BLK, BLK)
    here = pl.ds(at, BLK)
    h1 = n_in[...] * norm[0:1, :] + norm[3:4, :]
    n2, rstd2 = norm_forward(h1 + dot_nt(m_in[...], w_ref[0]))
    h2 = n2 * norm[1:2, :] + norm[4:5, :]
    h2b = h2.astype(BF)
    h_t[:, here] = h2b.T
    r3 = h2
    for b in range(blocks):
        act, slope = gelu_both(dot(h2b, w_ref[1 + b]))
        act = act.astype(BF)
        act_ref[b, here, :] = act
        slope_ref[b] = slope
        r3 = r3 + dot_nt(act, w_ref[1 + blocks + b])
    n3, rstd3 = norm_forward(r3)
    result = n3 * norm[2:3, :] + norm[5:6, :]
    own, oth = halves(meta, result.astype(BF))
    out_own[...] = own
    out_oth[...] = oth
    dy = natural(meta, cot_own[...], cot_oth[...]).astype(F32)
    dr3, gain3, bias3 = norm_backward(dy, n3, rstd3, norm[2:3, :])
    df = dr3.astype(BF)
    df_t[:, here] = df.T
    dh2 = dr3
    for b in range(blocks):
        dpre = (dot(df, w_ref[1 + blocks + b]) * slope_ref[b]).astype(BF)
        pre_ref[b, here, :] = dpre
        dh2 = dh2 + dot_nt(dpre, w_ref[1 + b])
    dr2, gain2, bias2 = norm_backward(dh2, n2, rstd2, norm[1:2, :])
    dr_ref[...] = dr2
    ng_ref[1:2, :] += gain2
    ng_ref[2:3, :] += gain3
    ng_ref[4:5, :] += bias2
    ng_ref[5:6, :] += bias3

    @pl.when(i == GRID - 1)
    def _():
        for b in range(blocks):
            put_grad(g_own, g_oth, b, dot(h_t[...], pre_ref[b]))
            put_grad(g_own, g_oth, blocks + b, dot(df_t[...], act_ref[b]))


def put_grad(g_own, g_oth, m, value):
    value = value.astype(BF)
    g_own[:, m] = value[:, :HALF].reshape(PIECES, CH, HALF)
    g_oth[:, m] = value[:, HALF:].reshape(PIECES, CH, HALF)


def ffn(meta, n1, m2, norm, cot_own, cot_oth, pieces):
    mats = pieces[0].shape[1]
    blocks = (mats - 1) // 2
    full = rows_spec(D)
    half = rows_spec(HALF)
    cot = pl.BlockSpec((BLK, HALF), lambda i, meta: (meta[CORE] * GRID + i, 0))
    grad = (PIECES, 2 * blocks, CH, HALF)
    return call(
        ffn_body,
        (GRID,),
        [full, full, fixed_spec((8, D)), cot, cot] + [ANY] * 8,
        (half, half, full, fixed_spec((D, D)), fixed_spec(grad), fixed_spec(grad), fixed_spec((8, D))),
        (sds((TOK, HALF)),) * 2
        + (sds((TOK, D), F32), sds((D, D)), sds(grad), sds(grad), sds((8, D), F32)),
        [
            pltpu.VMEM((mats, D, D), BF),
            pltpu.VMEM((blocks, TOK, D), BF),
            pltpu.VMEM((blocks, TOK, D), BF),
            pltpu.VMEM((blocks, BLK, D), F32),
            pltpu.VMEM((D, TOK), BF),
            pltpu.VMEM((D, TOK), BF),
            pltpu.SemaphoreType.DMA((8,)),
        ],
        flops=2 * TOK * D * D * (1 + 6 * blocks),
        nbytes=20 * 2**20,
    )(meta, n1, m2, norm, cot_own, cot_oth, *pieces)


def cross_backward_body(*refs):
    (meta, dr_in, m_in, p_in, q_in, k_in, v_in, e_in, h_in, n_in, r_in, norm, ng_in, w_ref, po_ref) = refs[:15]
    dr_ref, dk_ref, dv_ref, g_own, g_oth, ng_ref = refs[15:21]
    da_t, h_t, e_t, m_all, dq_all, dk_all, dv_all, dm_ref = refs[21:]
    i = pl.program_id(0)

    @pl.when(i == 0)
    def _():
        ng_ref[...] = ng_in[...]

    here = pl.ds(pl.multiple_of(i * BLK, BLK), BLK)
    dr2 = dr_in[...]
    da = dr2.astype(BF)
    da_t[:, here] = da.T
    h_t[:, here] = h_in[...].T
    e_t[:, here] = e_in[...].T
    m_all[here, :] = m_in[...]
    dm_ref[...] = dot(da, po_ref[...]).astype(BF)
    low, high = lane_masks()
    pick = low_lanes()
    for s in range(PER):
        rows = slice(s * PACK, (s + 1) * PACK)
        there = pl.ds(pl.multiple_of(i * BLK + s * PACK, PACK), PACK)
        for h in range(H // 2):
            cols = slice(h * PACK, (h + 1) * PACK)
            dq, dk, dv = pair_backward(
                q_in[rows, cols], k_in[rows, cols], v_in[rows, cols],
                p_in[s * (H // 2) + h], dm_ref[rows, cols], low, high, pick,
            )
            dq_all[there, cols] = dq
            dk_all[there, cols] = dk
            dv_all[there, cols] = dv
    dk_ref[...] = dk_all[here, :]
    dv_ref[...] = dv_all[here, :]
    dh1 = dr2 + dot_nt(dq_all[here, :], w_ref[1])
    dr1, gain1, bias1 = norm_backward(dh1, n_in[...], r_in[:, 0:1], norm[0:1, :])
    dr_ref[...] = dr1
    ng_ref[0:1, :] += gain1
    ng_ref[3:4, :] += bias1

    @pl.when(i == GRID - 1)
    def _():
        put_grad(g_own, g_oth, 0, dot(da_t[...], m_all[...]))
        put_grad(g_own, g_oth, 1, dot(h_t[...], dq_all[...]))
        put_grad(g_own, g_oth, 2, dot(e_t[...], dk_all[...]))
        put_grad(g_own, g_oth, 3, dot(e_t[...], dv_all[...]))
        total = jnp.concatenate([ng_ref[...], jnp.zeros((CH - 8, D), F32)], 0).astype(BF)
        for c in range(PIECES):
            part = total[:, :HALF] if c < PIECES // 2 else total[:, HALF:]
            g_own[c, 4] = part
            g_oth[c, 4] = part


def cross_backward(meta, dr2, m2, p2, q2, k2, v2, enc, h1, n1, rstd1, norm, ng, w, po):
    full = rows_spec(D)
    p_spec = pl.BlockSpec((PER * H // 2, 2 * PACK, PACK), lambda i, meta: (i, 0, 0))
    grad = (PIECES, 5, CH, HALF)
    small = fixed_spec((8, D))
    return call(
        cross_backward_body,
        (GRID,),
        [full, full, p_spec, full, full, full, full, full, full, rows_spec(PACK), small, small]
        + [fixed_spec((5, D, D)), fixed_spec((D, D))],
        (full, full, full, fixed_spec(grad), fixed_spec(grad), small),
        (sds((TOK, D), F32), sds((TOK, D)), sds((TOK, D)), sds(grad), sds(grad), sds((8, D), F32)),
        [pltpu.VMEM((D, TOK), BF)] * 3
        + [pltpu.VMEM((TOK, D), BF)] * 4
        + [pltpu.VMEM((BLK, D), BF)],
        flops=2 * TOK * D * D * 8,
        nbytes=20 * 2**20,
    )(meta, dr2, m2, p2, q2, k2, v2, enc, h1, n1, rstd1, norm, ng, w, po)


def self_backward_body(*refs):
    (meta, dr_in, m_in, p_in, q_in, k_in, v_in, x_in, po_ref) = refs[:9]
    dq_ref, dk_ref, dv_ref, g_own, g_oth = refs[9:14]
    da_t, x_t, m_all, dq_all, dk_all, dv_all, dm_ref = refs[14:]
    i = pl.program_id(0)
    here = pl.ds(pl.multiple_of(i * BLK, BLK), BLK)
    da = dr_in[...].astype(BF)
    da_t[:, here] = da.T
    x_t[:, here] = x_in[...].T
    m_all[here, :] = m_in[...]
    dm_ref[...] = dot(da, po_ref[0]).astype(BF)
    low, high = lane_masks()
    pick = low_lanes()
    for s in range(PER):
        rows = slice(s * PACK, (s + 1) * PACK)
        there = pl.ds(pl.multiple_of(i * BLK + s * PACK, PACK), PACK)
        for h in range(H // 2):
            cols = slice(h * PACK, (h + 1) * PACK)
            dq, dk, dv = pair_backward(
                q_in[rows, cols], k_in[rows, cols], v_in[rows, cols],
                p_in[s * (H // 2) + h], dm_ref[rows, cols], low, high, pick,
            )
            dq_all[there, cols] = dq
            dk_all[there, cols] = dk
            dv_all[there, cols] = dv
    dq_ref[...] = dq_all[here, :]
    dk_ref[...] = dk_all[here, :]
    dv_ref[...] = dv_all[here, :]

    @pl.when(i == GRID - 1)
    def _():
        put_grad(g_own, g_oth, 0, dot(da_t[...], m_all[...]))
        put_grad(g_own, g_oth, 1, dot(x_t[...], dq_all[...]))
        put_grad(g_own, g_oth, 2, dot(x_t[...], dk_all[...]))
        put_grad(g_own, g_oth, 3, dot(x_t[...], dv_all[...]))


def self_backward(meta, dr1, m, p, q, k, v, x, w_cross):
    full = rows_spec(D)
    p_spec = pl.BlockSpec((PER * H // 2, 2 * PACK, PACK), lambda i, meta: (i, 0, 0))
    grad = (PIECES, 4, CH, HALF)
    return call(
        self_backward_body,
        (GRID,),
        [full, full, p_spec, full, full, full, full, fixed_spec((1, D, D))],
        (full, full, full, fixed_spec(grad), fixed_spec(grad)),
        (sds((TOK, D)),) * 3 + (sds(grad), sds(grad)),
        [pltpu.VMEM((D, TOK), BF)] * 2
        + [pltpu.VMEM((TOK, D), BF)] * 4
        + [pltpu.VMEM((BLK, D), BF)],
        flops=2 * TOK * D * D * 6,
        nbytes=12 * 2**20,
    )(meta, dr1, m, p, q, k, v, x, w_cross)


def inputs_backward_body(meta, dr, dq, dk, dv, dk2, dv2, w_self, w_cross, x_own, x_oth, e_own, e_oth):
    dx = dr[...] + dot_nt(dq[...], w_self[0]) + dot_nt(dk[...], w_self[1]) + dot_nt(dv[...], w_self[2])
    x_own[...], x_oth[...] = halves(meta, dx.astype(BF))
    de = dot_nt(dk2[...], w_cross[2]) + dot_nt(dv2[...], w_cross[3])
    e_own[...], e_oth[...] = halves(meta, de.astype(BF))


def inputs_backward(meta, dr1, dq, dk, dv, dk2, dv2, w_self, w_cross):
    full = rows_spec(D)
    return call(
        inputs_backward_body,
        (GRID,),
        [full] * 6 + [fixed_spec((3, D, D)), fixed_spec((5, D, D))],
        (rows_spec(HALF),) * 4,
        (sds((TOK, HALF)),) * 4,
        flops=2 * TOK * D * D * 5,
        nbytes=14 * 2**20,
    )(meta, dr1, dq, dk, dv, dk2, dv2, w_self, w_cross)


def place_body(meta, own, oth, out, sems):
    me = meta[CORE]
    copies = []
    for side, src in enumerate((own, oth)):
        first = ROW + SLOTS * side
        for j in range(SLOTS):
            at = pl.multiple_of(meta[first + j] * PACK, PACK)
            copies.append(
                pltpu.make_async_copy(
                    src.at[pl.ds(j * PACK, PACK)], out.at[pl.ds(at, PACK)], sems.at[side * SLOTS + j]
                )
            )
    for c in copies:
        c.start()
    for c in copies:
        c.wait()


def place(meta, own, oth):
    return call(
        place_body,
        (1,),
        [ANY, ANY],
        ANY,
        sds((2 * TOK, HALF)),
        [pltpu.SemaphoreType.DMA((2 * SLOTS,))],
        nbytes=4 * 2**20,
    )(meta, own, oth)


def pair_sum_body(meta, *refs):
    for k in range(4):
        refs[8 + k][...] = (refs[k][...].astype(F32) + refs[4 + k][...].astype(F32)).astype(BF)


def pair_sum(meta, own, rec):
    _, mats, _, _ = own.shape
    block = (1, mats, CH, HALF)

    def pick(k):
        return pl.BlockSpec(block, lambda i, meta: (meta[PIECE + 4 * k + i], 0, 0, 0))

    out = pl.BlockSpec(block, lambda i, meta: (i, 0, 0, 0))
    return call(
        pair_sum_body,
        (4,),
        [pick(k) for k in range(4)] * 2,
        (out,) * 4,
        (sds((4, mats, CH, HALF)),) * 4,
        flops=10**6,
        nbytes=own.size * 6,
    )(meta, own, own, own, own, rec, rec, rec, rec)


def four_sum_body(a, b, c, d, *outs):
    for j in range(4):
        total = a[j].astype(F32) + b[j].astype(F32) + (c[j].astype(F32) + d[j].astype(F32))
        outs[j][...] = total.astype(BF)


def four_sum(a, b, c, d):
    return pl.pallas_call(
        four_sum_body,
        out_shape=(sds(a.shape[1:]),) * 4,
        cost_estimate=pl.CostEstimate(flops=10**6, bytes_accessed=a.size * 10, transcendentals=0),
        compiler_params=pltpu.CompilerParams(vmem_limit_bytes=56 * 1024 * 1024),
    )(a, b, c, d)


def adam(weight, first_old, second_old, grad, rate, decay):
    first_new = beta_first * first_old + (1.0 - beta_first) * grad
    second_new = beta_second * second_old + (1.0 - beta_second) * grad * grad
    first_hat = first_new / (1.0 - beta_first**STEP)
    second_hat = second_new / (1.0 - beta_second**STEP)
    updated = weight - rate * (first_hat / (jnp.sqrt(second_hat) + adam_epsilon) + decay * weight)
    return (first_new, second_new, updated)


def swap(value):
    return lax.ppermute(value, "narrow", [(0, 1), (1, 0)])


def peer(value, mask):
    return lax.ppermute(value, "wide", [(i, i ^ mask) for i in range(lax.axis_size("wide"))])


def gather_pieces(g):
    z = jnp.stack([g] + [peer(g, 4 * k) for k in (1, 2, 3)])
    own = [z] + [peer(z, k) for k in (1, 2, 3)]
    return own + [swap(a) for a in own]


def sum_pieces(meta, own, oth):
    s = pair_sum(meta, own, swap(oth))
    z = four_sum(s[0], *[peer(s[k], k) for k in (1, 2, 3)])
    rest = [peer(z[k], 4 * k) for k in (1, 2, 3)]
    return z[0].astype(F32) + rest[0].astype(F32) + (rest[1].astype(F32) + rest[2].astype(F32))


def local(
    tokens,
    encoded,
    cotangent,
    target_lengths,
    source_segments,
    send_rows,
    proj_in,
    proj_out,
    ffn_in,
    ffn_out,
    norm_par,
    proj_in_moment,
    proj_in_square,
    proj_out_moment,
    proj_out_square,
    ffn_in_moment,
    ffn_in_square,
    ffn_out_moment,
    ffn_out_square,
    norm_moment,
    norm_square,
):
    wide_count = lax.axis_size("wide")
    w = lax.axis_index("wide")
    n = lax.axis_index("narrow")
    rows_dev = tokens.shape[0] // PACK
    stride = wide_count // rows_dev
    share = proj_in.shape[1]
    blocks = ffn_in.shape[1] // HALF
    direct = share == CH

    places = jnp.arange(rows_dev, dtype=jnp.int32)
    slot_rows = lax.dynamic_index_in_dim(send_rows, w, 0, keepdims=False)[places * stride + w % stride]
    mine = lax.dynamic_slice_in_dim(slot_rows, n * SLOTS, SLOTS)
    theirs = lax.dynamic_slice_in_dim(slot_rows, (1 - n) * SLOTS, SLOTS)
    mine_global = w * rows_dev + mine
    lengths = target_lengths[mine_global]
    if direct:
        piece_ids = w ^ jnp.array([a | (b << 2) for a in range(4) for b in range(4)], jnp.int32)
    else:
        piece_ids = jnp.arange(PIECES, dtype=jnp.int32)
    meta = jnp.concatenate(
        [n[None], piece_ids, mine, theirs, lengths[:, 0], lengths[:, 0] + lengths[:, 1], mine_global]
    ).astype(jnp.int32)

    if direct:
        g0, g1, g2 = pack(proj_in, proj_out, ffn_in, ffn_out, norm_par)
        pieces = [gather_pieces(g) for g in (g0, g1, g2)]
    else:
        low_in = lax.all_gather(proj_in.astype(BF), "wide", axis=1, tiled=True)
        low_out = lax.all_gather(proj_out.astype(BF), "wide", axis=2, tiled=True).transpose(0, 2, 1)
        low_win = lax.all_gather(ffn_in.astype(BF), "wide", axis=0, tiled=True)
        low_wout = lax.all_gather(ffn_out.astype(BF), "wide", axis=1, tiled=True).T
        low_norm = lax.all_gather(norm_par.astype(BF), "wide", axis=1, tiled=True)

        def column_blocks(a):
            return a.reshape(D, blocks, HALF).transpose(1, 0, 2)

        tiled = jnp.tile(low_norm.reshape(6, PIECES, CH).transpose(1, 0, 2), (1, 1, HALF // CH))
        norm_mat = jnp.pad(tiled, ((0, 0), (0, CH - 6), (0, 0))).reshape(1, D, HALF)
        groups = (
            low_in[:3],
            jnp.concatenate([low_out[:1], low_in[3:], norm_mat]),
            jnp.concatenate([low_out[1:], column_blocks(low_win), column_blocks(low_wout)]),
        )
        pieces = []
        for group in groups:
            cut = group.reshape(-1, PIECES, CH, HALF).transpose(1, 0, 2, 3)
            own = [cut[4 * k : 4 * k + 4] for k in range(4)]
            pieces.append(own + [swap(a) for a in own])

    tok_oth = swap(tokens)
    enc_oth = swap(encoded)
    everyone = [[r + stride * j for j in range(rows_dev)] for r in range(stride)]

    def exchange(rows):
        return lax.all_to_all(
            rows.reshape(rows_dev, PACK, HALF), "wide", 0, 0, axis_index_groups=everyone
        ).reshape(rows_dev * PACK, HALF)

    cot_own = exchange(cotangent)
    cot_oth = swap(cot_own)
    segs = source_segments.reshape(-1, 1, PACK)

    x, q1, k1, v1, m1, p1, w_self = self_forward(meta, tokens, tok_oth, pieces[0])
    n1, rstd1, h1, enc, q2, k2, v2, m2, p2, w_cross, norm = cross_forward(
        meta, x, m1, encoded, enc_oth, segs, pieces[1]
    )
    out_own, out_oth, dr2, po2, gf_own, gf_oth, ng = ffn(
        meta, n1, m2, norm, cot_own, cot_oth, pieces[2]
    )
    dr1, dk2, dv2, gc_own, gc_oth, ng = cross_backward(
        meta, dr2, m2, p2, q2, k2, v2, enc, h1, n1, rstd1, norm, ng, w_cross, po2
    )
    dq1, dk1, dv1, gs_own, gs_oth = self_backward(meta, dr1, m1, p1, q1, k1, v1, x, w_cross)
    dx_own, dx_oth, de_own, de_oth = inputs_backward(
        meta, dr1, dq1, dk1, dv1, dk2, dv2, w_self, w_cross
    )
    tokens_grad = place(meta, dx_own, swap(dx_oth))
    encoded_grad = place(meta, de_own, swap(de_oth))

    out_rec = swap(out_oth)
    out_lo = jnp.where(n == 0, out_own, out_rec)
    out_hi = jnp.where(n == 0, out_rec, out_own)
    layer_out = exchange(jnp.concatenate([out_lo, out_hi], 0))

    if direct:
        gf = sum_pieces(meta, gf_own, gf_oth)
        gc = sum_pieces(meta, gc_own, gc_oth)
        gs = sum_pieces(meta, gs_own, gs_oth)
        norm_half = gc[4, :6]
        norm_grad = lax.dynamic_slice_in_dim(norm_half, (w % (HALF // CH)) * CH, CH, 1)
    else:

        def summed(own, oth):
            total = (own.astype(F32) + swap(oth).astype(F32)).astype(BF)
            total = total.transpose(1, 0, 2, 3).reshape(-1, D, HALF)
            return lax.psum_scatter(total, "wide", scatter_dimension=1, tiled=True).astype(F32)

        gf, gc, gs = summed(gf_own, gf_oth), summed(gc_own[:, :4], gc_oth[:, :4]), summed(gs_own, gs_oth)
        norm_all = lax.psum(ng, ("wide", "narrow"))[:6]
        norm_grad = lax.dynamic_slice_in_dim(norm_all, w * share, share, 1)

    grad_in = jnp.concatenate([gs[1:4], gc[1:4]])
    grad_out = jnp.stack([gs[0], gc[0]]).transpose(0, 2, 1)
    grad_expand = gf[:blocks].transpose(1, 0, 2).reshape(share, blocks * HALF)
    grad_reduce = gf[blocks:].transpose(1, 0, 2).reshape(share, blocks * HALF).T
    upd_in = adam(proj_in, proj_in_moment, proj_in_square, grad_in, rate_matrix, decay_matrix)
    upd_out = adam(proj_out, proj_out_moment, proj_out_square, grad_out, rate_matrix, decay_matrix)
    upd_expand = adam(ffn_in, ffn_in_moment, ffn_in_square, grad_expand, rate_matrix, decay_matrix)
    upd_reduce = adam(ffn_out, ffn_out_moment, ffn_out_square, grad_reduce, rate_matrix, decay_matrix)
    upd_norm = adam(norm_par, norm_moment, norm_square, norm_grad, rate_norm, 0.0)
    return (layer_out, tokens_grad, encoded_grad) + upd_in + upd_out + upd_expand + upd_reduce + upd_norm


def solution(mesh):
    rows = P("wide", "narrow")
    p_in = P(None, "wide", "narrow")
    p_out = P(None, "narrow", "wide")
    p_expand = P("wide", "narrow")
    p_reduce = P("narrow", "wide")
    p_norm = P(None, "wide")
    weights = (p_in, p_out, p_expand, p_reduce, p_norm)
    in_specs = (rows,) * 3 + (P(),) * 3 + weights + tuple(s for s in weights for _ in range(2))
    out_specs = (rows,) * 3 + tuple(s for s in weights for _ in range(3))
    return jax.shard_map(local, mesh=mesh, in_specs=in_specs, out_specs=out_specs, check_vma=False)
```

time: 1040 us -> 391 us (0.38)
  waiting for transfers between devices: 449 us -> 94.2 us
  Pallas kernels: 0 us -> 192 us
  blocking collectives: 160 us -> 0 us
  matrix products: 119 us -> 0 us
  local copies, waits for them, and re-layouts: 117 us -> 11.8 us
  other arithmetic: 58.4 us -> 9.95 us
  starting transfers between devices: 109 us -> 80.8 us
  between operations: 15.7 us -> 1.41 us
    pallas_call x0 -> x15, Pallas kernels: none -> 192 us  [the longest x2 67.5 us: place(): call(place_body, (1,), [ANY, ANY], ANY, sds((2 * TOK, HALF)), [pltpu.Sema...]
    ppermute x60 -> x57, waiting for transfers between devices: 222 us -> 94.2 us  [the longest x36 93 us: peer(): lax.ppermute(value, 'wide', [(i, i ^ mask) for i in range(lax.axis_size('...]
    psum x7 -> x0, waiting for transfers between devices: 122 us -> none  [the longest x6 104 us: add_branch(): return base + lax.psum(partial_sum, 'narrow')]
    dot_general x86 -> x0, matrix products: 119 us -> none  [the longest x10 37 us: matmul(): return jnp.dot(left_side, right_side, preferred_element_type=jnp.float32)]
    all_gather x6 -> x0, waiting for transfers between devices: 103 us -> none  [the longest x1 52.6 us: local(): lax.all_gather(ffn_in.astype(jnp.bfloat16), 'wide', axis=0, tiled=True)]
    all_gather x2 -> x0, blocking collectives: 83 us -> none  [the longest x1 44.9 us: local(): lax.all_gather(proj_out.astype(jnp.bfloat16), 'wide', axis=2, tiled=True)]
    psum x1 -> x0, blocking collectives: 77.4 us -> none  [local(): lax.psum((local_grads[0], local_grads[1], local_grads[2], local_grads[3],...]
    dynamic_slice x59 -> x0, local copies, waits for them, and re-layouts: 48.8 us -> none  [the longest x56 48.6 us: attend_forward(): lax.map(single, (query_rows, key_rows, value_rows, seg_query, seg_key))]
  transfers between devices with their start and end apart: 74 -> 59, of which waited for: 49 -> 15; matrix products, arithmetic and copies ran while one was open for 17% -> 3% of each run, Pallas kernels for 0% -> 42%
where the time goes in v1:
time: 391 us; the launch traced here: 390 us
  Pallas kernels  192 us (49%)
  waiting for transfers between devices  94.2 us (24%)
  starting transfers between devices  80.8 us (21%)
  local copies, waits for them, and re-layouts  11.8 us (3%)
  other arithmetic  9.95 us (3%)
    ppermute x36, waiting for transfers between devices, peer(): lax.ppermute(value, 'wide', [(i, i ^ mask) for i in range(lax.axis_size('...  93 us
    pallas_call x2, Pallas kernels, place(): call(place_body, (1,), [ANY, ANY], ANY, sds((2 * TOK, HALF)), [pltpu.Sema...  67.5 us
    ppermute x36, starting transfers between devices, peer(): lax.ppermute(value, 'wide', [(i, i ^ mask) for i in range(lax.axis_size('...  62.2 us
    pallas_call x1, Pallas kernels, ffn(): call(ffn_body, (GRID,), [full, full, fixed_spec((8, D)), cot, cot] + [ANY...  29.7 us
    pallas_call x1, Pallas kernels, cross_backward(): call(cross_backward_body, (GRID,), [full, full, p_spec, full, full, full,...  21.2 us
    pallas_call x1, Pallas kernels, self_backward(): call(self_backward_body, (GRID,), [full, full, p_spec, full, full, full,...  18.7 us
    all_to_all x2, starting transfers between devices, exchange(): lax.all_to_all(rows.reshape(rows_dev, PACK, HALF), 'wide', 0, 0, axis_ind...  14 us
    pallas_call x3, Pallas kernels, pair_sum(): call(pair_sum_body, (4,), [pick(k) for k in range(4)] * 2, (out,) * 4, (s...  14 us
  transfers between devices with their start and end apart: 59, of which 15 were waited for; matrix products, arithmetic and copies ran while one was open for 3% of the time, Pallas kernels for 42%

profile of v1, /device:TPU:0, one launch (start us, length us, event | category | flops | bytes accessed | tf_op | source)
XLA Modules:
  0.0 389.7 jit_solution(393562188936654482)
XLA Ops:
  0.7 8.5 %all-to-all-start = ((bf16[16,128,256]{2,1,0:T(8,128)(2,1)}), bf16[16,128,256]{2,1,0:T(8,128)(2,1)S(1)}, u32[]{:S(2)}, u32[]{:S(2)}) async-start(bf16[16,128,256]{2,1,0:T(8,128)(2,1)} %bitcast.51), calls=%async_computation | async-start | bytes 2097152 | tf_op jit(solution)/shard_map/all_to_all | solution.py:751
  17.6 3.7 collective-permute-start.14
  21.4 7.1 %collective-permute-done.1 = bf16[3,32,256]{2,1,0:T(8,128)(2,1)S(1)} collective-permute-done((bf16[3,32,256]{2,1,0:T(8,128)(2,1)}, bf16[3,32,256]{2,1,0:T(8,128)(2,1)S(1)}, u32[]{:S(2)}, u32[]{:S(2)}) %collective-permute-start.1) | collective-permute-done | bytes 49184 | tf_op jit(solution)/shard_map/ppermute | solution.py:658
  28.5 4.7 %collective-permute-start.13 = (bf16[5,32,256]{2,1,0:T(8,128)(2,1)}, bf16[5,32,256]{2,1,0:T(8,128)(2,1)S(1)}, u32[]{:S(2)}, u32[]{:S(2)}) collective-permute-start(bf16[5,32,256]{2,1,0:T(8,128)(2,1)} %get-tuple-element.87), channel_id=1, source_target_pairs={{0,16},{2,18},{4,20},{6,22},{8,24},{10,26},{12,28},{14,30},{16,0},... | collective-permute-start | bytes 245768 | tf_op jit(solution)/shard_map/ppermute | solution.py:658
  33.2 9.4 %collective-permute-done.2 = bf16[3,32,256]{2,1,0:T(8,128)(2,1)S(1)} collective-permute-done((bf16[3,32,256]{2,1,0:T(8,128)(2,1)}, bf16[3,32,256]{2,1,0:T(8,128)(2,1)S(1)}, u32[]{:S(2)}, u32[]{:S(2)}) %collective-permute-start.2) | collective-permute-done | bytes 49184 | tf_op jit(solution)/shard_map/ppermute | solution.py:658
  47.6 2.7 collective-permute-start.25
  53.8 4.3 %collective-permute-done.24 = bf16[9,32,256]{2,1,0:T(8,128)(2,1)S(1)} collective-permute-done((bf16[9,32,256]{2,1,0:T(8,128)(2,1)}, bf16[9,32,256]{2,1,0:T(8,128)(2,1)S(1)}, u32[]{:S(2)}, u32[]{:S(2)}) %collective-permute-start.24) | collective-permute-done | bytes 147488 | tf_op jit(solution)/shard_map/ppermute | solution.py:658
  62.5 4.4 %collective-permute-done.15.refs_10_ = bf16[4,5,32,256]{3,2,1,0:T(8,128)(2,1)S(1)} collective-permute-done((bf16[4,5,32,256]{3,2,1,0:T(8,128)(2,1)S(1)}, bf16[4,5,32,256]{3,2,1,0:T(8,128)(2,1)S(1)}, u32[]{:S(2)}, u32[]{:S(2)}) %collective-permute-start.15) | collective-permute-done | bytes 327712 | tf_op jit(solution)/shard_map/ppermute | solution.py:658
  66.9 5.9 %collective-permute-done.16.refs_11_ = bf16[4,5,32,256]{3,2,1,0:T(8,128)(2,1)S(1)} collective-permute-done((bf16[4,5,32,256]{3,2,1,0:T(8,128)(2,1)S(1)}, bf16[4,5,32,256]{3,2,1,0:T(8,128)(2,1)S(1)}, u32[]{:S(2)}, u32[]{:S(2)}) %collective-permute-start.16) | collective-permute-done | bytes 327712 | tf_op jit(solution)/shard_map/ppermute | solution.py:658
  81.4 10.1 %collective-permute-done.26.refs_7_ = bf16[4,9,32,256]{3,2,1,0:T(8,128)(2,1)} collective-permute-done((bf16[4,9,32,256]{3,2,1,0:T(8,128)(2,1)S(1)}, bf16[4,9,32,256]{3,2,1,0:T(8,128)(2,1)}, u32[]{:S(2)}, u32[]{:S(2)}) %collective-permute-start.26) | collective-permute-done | bytes 589856 | tf_op jit(solution)/shard_map/ppermute | solution.py:658
  93.3 13.5 %collective-permute-done.27.refs_8_ = bf16[4,9,32,256]{3,2,1,0:T(8,128)(2,1)} collective-permute-done((bf16[4,9,32,256]{3,2,1,0:T(8,128)(2,1)S(1)}, bf16[4,9,32,256]{3,2,1,0:T(8,128)(2,1)}, u32[]{:S(2)}, u32[]{:S(2)}) %collective-permute-start.27) | collective-permute-done | bytes 589856 | tf_op jit(solution)/shard_map/ppermute | solution.py:658
  108.4 9.7 %shard_map.350 = (bf16[1024,512]{1,0:T(8,128)(2,1)}, bf16[1024,512]{1,0:T(8,128)(2,1)}, bf16[1024,512]{1,0:T(8,128)(2,1)}, bf16[1024,512]{1,0:T(8,128)(2,1)}, bf...) custom-call(s32[57]{0:T(128)} %concatenate.9.refs_0_.meta, ...), custom_call_target="tpu_custom_call" | custom-call | flops 2147483648 | bytes 10485760 | tf_op jit(solution)/shard_map/pallas_call | solution.py:244
  118.1 13.3 %shard_map.351 = (f32[1024,512]{1,0:T(8,128)}, f32[1024,128]{1,0:T(8,128)}, bf16[1024,512]{1,0:T(8,128)(2,1)}, bf16[1024,512]{1,0:T(8,128)(2,1)}, bf16[1024,512]...) custom-call(s32[57]{0:T(128)} %concatenate.9.refs_0_.meta, ...), custom_call_target="tpu_custom_call" | custom-call | flops 2684354560 | bytes 16777216 | tf_op jit(solution)/shard_map/pallas_call | solution.py:312
  132.3 29.7 %shard_map.352 = (bf16[1024,256]{1,0:T(8,128)(2,1)}, bf16[1024,256]{1,0:T(8,128)(2,1)}, f32[1024,512]{1,0:T(8,128)}, bf16[512,512]{1,0:T(8,128)(2,1)}, bf16[16,8...) custom-call(s32[57]{0:T(128)} %concatenate.9.refs_0_.meta, ...), custom_call_target="tpu_custom_call" | custom-call | flops 13421772800 | bytes 20971520 | tf_op jit(solution)/shard_map/pallas_call | solution.py:406
  162.2 21.2 %shard_map.353 = (f32[1024,512]{1,0:T(8,128)}, bf16[1024,512]{1,0:T(8,128)(2,1)}, bf16[1024,512]{1,0:T(8,128)(2,1)}, bf16[16,5,32,256]{3,2,1,0:T(8,128)(2,1)}, b...) custom-call(s32[57]{0:T(128)} %concatenate.9.refs_0_.meta, f32[1024,512]{1,0:T(8,128)} %get-tuple-element.94.refs_1_, ...), custom_call_target="tpu_custom_call" | custom-call | flops 4294967296 | bytes 20971520 | tf_op jit(solution)/shard_map/pallas_call | solution.py:485
  183.9 18.7 %shard_map.354 = (bf16[1024,512]{1,0:T(8,128)(2,1)}, bf16[1024,512]{1,0:T(8,128)(2,1)}, bf16[1024,512]{1,0:T(8,128)(2,1)}, bf16[16,4,32,256]{3,2,1,0:T(8,128)(2,1)}, bf16[16,4,32,256]{3,2,1,0:T(8,128)(2,1)}) custom-call(s32[57]{0:T(128)} %concatenate.9.refs_0_.meta, f32[1024,512]{1,0:T(8,128)} %get-tuple-element.105.refs_1_.dr, ...), custom_call_target="tpu_custom_call" | custom-call | flops 3221225472 | bytes 12582912 | tf_op jit(solution)/shard_map/pallas_call | solution.py:541
  203.1 8.8 %shard_map.355 = (bf16[1024,256]{1,0:T(8,128)(2,1)}, bf16[1024,256]{1,0:T(8,128)(2,1)}, bf16[1024,256]{1,0:T(8,128)(2,1)}, bf16[1024,256]{1,0:T(8,128)(2,1)}) custom-call(s32[57]{0:T(128)} %concatenate.9.refs_0_.meta, f32[1024,512]{1,0:T(8,128)} %get-tuple-element.105.refs_1_.dr, bf16[1024,512]{1,0:T(8,128)(2,1)} %get-tuple-element.110.dq, ...), custom_call_target="tpu_custom_call" | custom-call | flops 2684354560 | bytes 14680064 | tf_op jit(solution)/shard_map/pallas_call | solution.py:564
  214.2 5.6 %all-to-all-start.1 = ((bf16[16,128,256]{2,1,0:T(8,128)(2,1)}), bf16[16,128,256]{2,1,0:T(8,128)(2,1)}, u32[]{:S(2)}, u32[]{:S(2)}) async-start(bf16[16,128,256]{2,1,0:T(8,128)(2,1)} %bitcast.50), calls=%async_computation.1 | async-start | bytes 2097152 | tf_op jit(solution)/shard_map/all_to_all | solution.py:751
  219.8 4.4 %shard_map.358 = (bf16[4,4,32,256]{3,2,1,0:T(8,128)(2,1)}, bf16[4,4,32,256]{3,2,1,0:T(8,128)(2,1)}, bf16[4,4,32,256]{3,2,1,0:T(8,128)(2,1)}, bf16[4,4,32,256]{3,2,1,0:T(8,128)(2,1)}) custom-call(s32[57]{0:T(128)} %concatenate.9.refs_0_.meta, bf16[16,4,32,256]{3,2,1,0:T(8,128)(2,1)} %get-tuple-element.120.refs_0_.refs_1_.refs_2_.refs_3_, ...), custom_call_target="tpu_custom_call" | custom-call | flops 1000000 | bytes 3145728 | tf_op jit(solution)/shard_map/pallas_call | solution.py:618
  228.8 4.5 %shard_map.360 = (bf16[4,5,32,256]{3,2,1,0:T(8,128)(2,1)}, bf16[4,5,32,256]{3,2,1,0:T(8,128)(2,1)}, bf16[4,5,32,256]{3,2,1,0:T(8,128)(2,1)}, bf16[4,5,32,256]{3,2,1,0:T(8,128)(2,1)}) custom-call(s32[57]{0:T(128)} %concatenate.9.refs_0_.meta, bf16[16,5,32,256]{3,2,1,0:T(8,128)(2,1)} %get-tuple-element.130.refs_0_.refs_1_.refs_2_.refs_3_, ...), custom_call_target="tpu_custom_call" | custom-call | flops 1000000 | bytes 3932160 | tf_op jit(solution)/shard_map/pallas_call | solution.py:618
  233.3 6.0 %collective-permute-done.37.b = bf16[4,4,32,256]{3,2,1,0:T(8,128)(2,1)S(1)} collective-permute-done((bf16[4,4,32,256]{3,2,1,0:T(8,128)(2,1)}, bf16[4,4,32,256]{3,2,1,0:T(8,128)(2,1)S(1)}, u32[]{:S(2)}, u32[]{:S(2)}) %collective-permute-start.37) | collective-permute-done | bytes 262176 | tf_op jit(solution)/shard_map/ppermute | solution.py:658
  242.6 6.8 %collective-permute-done.39.d = bf16[4,4,32,256]{3,2,1,0:T(8,128)(2,1)S(1)} collective-permute-done((bf16[4,4,32,256]{3,2,1,0:T(8,128)(2,1)}, bf16[4,4,32,256]{3,2,1,0:T(8,128)(2,1)S(1)}, u32[]{:S(2)}, u32[]{:S(2)}) %collective-permute-start.39) | collective-permute-done | bytes 262176 | tf_op jit(solution)/shard_map/ppermute | solution.py:658
  254.7 2.8 collective-permute-start.41
  257.5 7.2 %collective-permute-start.42 = (bf16[4,32,256]{2,1,0:T(8,128)(2,1)}, bf16[4,32,256]{2,1,0:T(8,128)(2,1)S(1)}, u32[]{:S(2)}, u32[]{:S(2)}) collective-permute-start(bf16[4,32,256]{2,1,0:T(8,128)(2,1)} %get-tuple-element.129), channel_id=1, source_target_pairs={{0,24},{2,26},{4,28},{6,30},{8,16},{10,18},{12,20},{14,22},{16,8},... | collective-permute-start | bytes 196616 | tf_op jit(solution)/shard_map/ppermute | solution.py:658
  264.7 33.7 %shard_map.357 = bf16[2048,256]{1,0:T(8,128)(2,1)} custom-call(s32[57]{0:T(128)} %concatenate.9.refs_0_.meta, bf16[1024,256]{1,0:T(8,128)(2,1)} %get-tuple-element.118.own, bf16[1024,256]{1,0:T(8,128)(2,1)} %collective-permute-done.35.oth), custom_call_target="tpu_custom_call" | custom-call | bytes 4194304 | tf_op jit(solution)/shard_map/pallas_call | solution.py:594
  298.4 33.8 %shard_map.356 = bf16[2048,256]{1,0:T(8,128)(2,1)} custom-call(s32[57]{0:T(128)} %concatenate.9.refs_0_.meta, bf16[1024,256]{1,0:T(8,128)(2,1)} %get-tuple-element.116.own, bf16[1024,256]{1,0:T(8,128)(2,1)} %collective-permute-done.34.oth), custom_call_target="tpu_custom_call" | custom-call | bytes 4194304 | tf_op jit(solution)/shard_map/pallas_call | solution.py:594
  335.6 3.8 collective-permute-start.49
  340.9 5.1 %shard_map.362 = (bf16[4,8,32,256]{3,2,1,0:T(8,128)(2,1)}, bf16[4,8,32,256]{3,2,1,0:T(8,128)(2,1)}, bf16[4,8,32,256]{3,2,1,0:T(8,128)(2,1)}, bf16[4,8,32,256]{3,2,1,0:T(8,128)(2,1)}) custom-call(s32[57]{0:T(128)} %concatenate.9.refs_0_.meta, bf16[16,8,32,256]{3,2,1,0:T(8,128)(2,1)} %get-tuple-element.140.refs_0_.refs_1_.refs_2_.refs_3_, ...), custom_call_target="tpu_custom_call" | custom-call | flops 1000000 | bytes 6291456 | tf_op jit(solution)/shard_map/pallas_call | solution.py:618
  351.3 9.8 %collective-permute-done.51.b = bf16[4,8,32,256]{3,2,1,0:T(8,128)(2,1)S(1)} collective-permute-done((bf16[4,8,32,256]{3,2,1,0:T(8,128)(2,1)}, bf16[4,8,32,256]{3,2,1,0:T(8,128)(2,1)S(1)}, u32[]{:S(2)}, u32[]{:S(2)}) %collective-permute-start.51) | collective-permute-done | bytes 524320 | tf_op jit(solution)/shard_map/ppermute | solution.py:658
  361.1 9.5 %collective-permute-done.53.d = bf16[4,8,32,256]{3,2,1,0:T(8,128)(2,1)S(1)} collective-permute-done((bf16[4,8,32,256]{3,2,1,0:T(8,128)(2,1)}, bf16[4,8,32,256]{3,2,1,0:T(8,128)(2,1)S(1)}, u32[]{:S(2)}, u32[]{:S(2)}) %collective-permute-start.53) | collective-permute-done | bytes 524320 | tf_op jit(solution)/shard_map/ppermute | solution.py:658
  374.8 3.5 collective-permute-start.56
  380.7 4.0 %collective-permute-done.55 = bf16[8,32,256]{2,1,0:T(8,128)(2,1)S(1)} collective-permute-done((bf16[8,32,256]{2,1,0:T(8,128)(2,1)}, bf16[8,32,256]{2,1,0:T(8,128)(2,1)S(1)}, u32[]{:S(2)}, u32[]{:S(2)}) %collective-permute-start.55) | collective-permute-done | bytes 131104 | tf_op jit(solution)/shard_map/ppermute | solution.py:658
  (247 shorter events, 72.2 us)
Async XLA Ops:
  0.7 90.9 %all-to-all-start = ((bf16[16,128,256]{2,1,0:T(8,128)(2,1)}), bf16[16,128,256]{2,1,0:T(8,128)(2,1)S(1)}, u32[]{:S(2)}, u32[]{:S(2)}) async-start(bf16[16,128,256]{2,1,0:T(8,128)(2,1)} %bitcast.51), calls=%async_computation | async-start | bytes 2097152 | tf_op jit(solution)/shard_map/all_to_all | solution.py:751
  15.2 27.4 %collective-permute-start.2 = (bf16[3,32,256]{2,1,0:T(8,128)(2,1)}, bf16[3,32,256]{2,1,0:T(8,128)(2,1)S(1)}, u32[]{:S(2)}, u32[]{:S(2)}) collective-permute-start(bf16[3,32,256]{2,1,0:T(8,128)(2,1)} %get-tuple-element.84), channel_id=1, source_target_pairs={{0,16},{2,18},{4,20},{6,22},{8,24},{10,26},{12,28},{14,30},{16,0},... | collective-permute-start | bytes 147464 | tf_op jit(solution)/shard_map/ppermute | solution.py:658
  17.5 25.0 %collective-permute-start.3 = (bf16[3,32,256]{2,1,0:T(8,128)(2,1)}, bf16[3,32,256]{2,1,0:T(8,128)(2,1)S(1)}, u32[]{:S(2)}, u32[]{:S(2)}) collective-permute-start(bf16[3,32,256]{2,1,0:T(8,128)(2,1)} %get-tuple-element.84), channel_id=1, source_target_pairs={{0,24},{2,26},{4,28},{6,30},{8,16},{10,18},{12,20},{14,22},{16,8},... | collective-permute-start | bytes 147464 | tf_op jit(solution)/shard_map/ppermute | solution.py:658
  17.6 28.3 %collective-permute-start.14 = (bf16[5,32,256]{2,1,0:T(8,128)(2,1)}, bf16[5,32,256]{2,1,0:T(8,128)(2,1)S(1)}, u32[]{:S(2)}, u32[]{:S(2)}) collective-permute-start(bf16[5,32,256]{2,1,0:T(8,128)(2,1)} %get-tuple-element.87), channel_id=1, source_target_pairs={{0,24},{2,26},{4,28},{6,30},{8,16},{10,18},{12,20},{14,22},{16,8},... | collective-permute-start | bytes 245768 | tf_op jit(solution)/shard_map/ppermute | solution.py:658
  21.4 26.2 %collective-permute-start.12 = (bf16[5,32,256]{2,1,0:T(8,128)(2,1)}, bf16[5,32,256]{2,1,0:T(8,128)(2,1)S(1)}, u32[]{:S(2)}, u32[]{:S(2)}) collective-permute-start(bf16[5,32,256]{2,1,0:T(8,128)(2,1)} %get-tuple-element.87), channel_id=1, source_target_pairs={{0,8},{2,10},{4,12},{6,14},{8,0},{10,2},{12,4},{14,6},{16,24},{18,... | collective-permute-start | bytes 245768 | tf_op jit(solution)/shard_map/ppermute | solution.py:658
  28.5 21.9 %collective-permute-start.13 = (bf16[5,32,256]{2,1,0:T(8,128)(2,1)}, bf16[5,32,256]{2,1,0:T(8,128)(2,1)S(1)}, u32[]{:S(2)}, u32[]{:S(2)}) collective-permute-start(bf16[5,32,256]{2,1,0:T(8,128)(2,1)} %get-tuple-element.87), channel_id=1, source_target_pairs={{0,16},{2,18},{4,20},{6,22},{8,24},{10,26},{12,28},{14,30},{16,0},... | collective-permute-start | bytes 245768 | tf_op jit(solution)/shard_map/ppermute | solution.py:658
  43.4 16.4 %collective-permute-start.6 = (bf16[4,3,32,256]{3,2,1,0:T(8,128)(2,1)S(1)}, bf16[4,3,32,256]{3,2,1,0:T(8,128)(2,1)S(1)}, u32[]{:S(2)}, u32[]{:S(2)}) collective-permute-start(bf16[4,3,32,256]{3,2,1,0:T(8,128)(2,1)S(1)} %pad_maximum_fusion.3.refs_5_), channel_id=1, source_target_pairs={{0,6},{2,4},{4,2},{6,0},{8,14},{10,12},{12,10},{14,8},{16,22},{18,... | collective-permute-start | bytes 589832 | tf_op jit(solution)/shard_map/ppermute | solution.py:658
  72.8 34.4 %collective-permute-start = (bf16[2048,256]{1,0:T(8,128)(2,1)S(1)}, bf16[2048,256]{1,0:T(8,128)(2,1)}, u32[]{:S(2)}, u32[]{:S(2)}) collective-permute-start(bf16[2048,256]{1,0:T(8,128)(2,1)S(1)} %copy-done.37), channel_id=1, source_target_pairs={{0,1},{1,0},{2,3},{3,2},{4,5},{5,4},{6,7},{7,6},{8,9},{9,8},{10,11... | collective-permute-start | bytes 3145736 | tf_op jit(solution)/shard_map/ppermute | solution.py:654
  73.4 33.9 %collective-permute-start.11 = (bf16[2048,256]{1,0:T(8,128)(2,1)}, bf16[2048,256]{1,0:T(8,128)(2,1)}, u32[]{:S(2)}, u32[]{:S(2)}) collective-permute-start(bf16[2048,256]{1,0:T(8,128)(2,1)} %refs_5_.1), channel_id=1, source_target_pairs={{0,1},{1,0},{2,3},{3,2},{4,5},{5,4},{6,7},{7,6},{8,9},{9,8},{10,11... | collective-permute-start | bytes 3145736 | tf_op jit(solution)/shard_map/ppermute | solution.py:654
  75.2 16.3 %collective-permute-start.26 = (bf16[4,9,32,256]{3,2,1,0:T(8,128)(2,1)S(1)}, bf16[4,9,32,256]{3,2,1,0:T(8,128)(2,1)}, u32[]{:S(2)}, u32[]{:S(2)}) collective-permute-start(bf16[4,9,32,256]{3,2,1,0:T(8,128)(2,1)S(1)} %pad_maximum_fusion.1.refs_6_), channel_id=1, source_target_pairs={{0,2},{2,0},{4,6},{6,4},{8,10},{10,8},{12,14},{14,12},{16,18},{18,... | collective-permute-start | bytes 1769480 | tf_op jit(solution)/shard_map/ppermute | solution.py:658
  78.4 28.4 %collective-permute-start.27 = (bf16[4,9,32,256]{3,2,1,0:T(8,128)(2,1)S(1)}, bf16[4,9,32,256]{3,2,1,0:T(8,128)(2,1)}, u32[]{:S(2)}, u32[]{:S(2)}) collective-permute-start(bf16[4,9,32,256]{3,2,1,0:T(8,128)(2,1)S(1)} %pad_maximum_fusion.1.refs_6_), channel_id=1, source_target_pairs={{0,4},{2,6},{4,0},{6,2},{8,12},{10,14},{12,8},{14,10},{16,20},{18,... | collective-permute-start | bytes 1769480 | tf_op jit(solution)/shard_map/ppermute | solution.py:658
  79.6 27.1 %collective-permute-start.28 = (bf16[4,9,32,256]{3,2,1,0:T(8,128)(2,1)S(1)}, bf16[4,9,32,256]{3,2,1,0:T(8,128)(2,1)}, u32[]{:S(2)}, u32[]{:S(2)}) collective-permute-start(bf16[4,9,32,256]{3,2,1,0:T(8,128)(2,1)S(1)} %pad_maximum_fusion.1.refs_6_), channel_id=1, source_target_pairs={{0,6},{2,4},{4,2},{6,0},{8,14},{10,12},{12,10},{14,8},{16,22},{18,... | collective-permute-start | bytes 1769480 | tf_op jit(solution)/shard_map/ppermute | solution.py:658
  91.6 40.0 %collective-permute-start.22 = (bf16[2048,256]{1,0:T(8,128)(2,1)S(1)}, bf16[2048,256]{1,0:T(8,128)(2,1)}, u32[]{:S(2)}, u32[]{:S(2)}) collective-permute-start(bf16[2048,256]{1,0:T(8,128)(2,1)S(1)} %bitcast.52), channel_id=1, source_target_pairs={{0,1},{1,0},{2,3},{3,2},{4,5},{5,4},{6,7},{7,6},{8,9},{9,8},{10,11... | collective-permute-start | bytes 3145736 | tf_op jit(solution)/shard_map/ppermute | solution.py:654
  106.7 24.7 %collective-permute-start.29 = (bf16[4,9,32,256]{3,2,1,0:T(8,128)(2,1)S(1)}, bf16[4,9,32,256]{3,2,1,0:T(8,128)(2,1)}, u32[]{:S(2)}, u32[]{:S(2)}) collective-permute-start(bf16[4,9,32,256]{3,2,1,0:T(8,128)(2,1)S(1)} %pad_maximum_fusion.1.refs_6_), channel_id=1, source_target_pairs={{0,1},{1,0},{2,3},{3,2},{4,5},{5,4},{6,7},{7,6},{8,9},{9,8},{10,11... | collective-permute-start | bytes 1769480 | tf_op jit(solution)/shard_map/ppermute | solution.py:654
  106.7 24.7 %collective-permute-start.30 = (bf16[4,9,32,256]{3,2,1,0:T(8,128)(2,1)}, bf16[4,9,32,256]{3,2,1,0:T(8,128)(2,1)}, u32[]{:S(2)}, u32[]{:S(2)}) collective-permute-start(bf16[4,9,32,256]{3,2,1,0:T(8,128)(2,1)} %collective-permute-done.26.refs_7_), channel_id=1, source_target_pairs={{0,1},{1,0},{2,3},{3,2},{4,5},{5,4},{6,7},{7,6},{8,9},{9,8},{10,11... | collective-permute-start | bytes 1769480 | tf_op jit(solution)/shard_map/ppermute | solution.py:654
  107.2 24.2 %collective-permute-start.31 = (bf16[4,9,32,256]{3,2,1,0:T(8,128)(2,1)}, bf16[4,9,32,256]{3,2,1,0:T(8,128)(2,1)S(1)}, u32[]{:S(2)}, u32[]{:S(2)}) collective-permute-start(bf16[4,9,32,256]{3,2,1,0:T(8,128)(2,1)} %collective-permute-done.27.refs_8_), channel_id=1, source_target_pairs={{0,1},{1,0},{2,3},{3,2},{4,5},{5,4},{6,7},{7,6},{8,9},{9,8},{10,11... | collective-permute-start | bytes 1769480 | tf_op jit(solution)/shard_map/ppermute | solution.py:654
  107.3 24.2 %collective-permute-start.32 = (bf16[4,9,32,256]{3,2,1,0:T(8,128)(2,1)}, bf16[4,9,32,256]{3,2,1,0:T(8,128)(2,1)}, u32[]{:S(2)}, u32[]{:S(2)}) collective-permute-start(bf16[4,9,32,256]{3,2,1,0:T(8,128)(2,1)} %collective-permute-done.28.refs_9_), channel_id=1, source_target_pairs={{0,1},{1,0},{2,3},{3,2},{4,5},{5,4},{6,7},{7,6},{8,9},{9,8},{10,11... | collective-permute-start | bytes 1769480 | tf_op jit(solution)/shard_map/ppermute | solution.py:654
  162.0 177.5 %collective-permute-start.50 = (bf16[16,8,32,256]{3,2,1,0:T(8,128)(2,1)}, bf16[16,8,32,256]{3,2,1,0:T(8,128)(2,1)S(1)}, u32[]{:S(2)}, u32[]{:S(2)}) collective-permute-start(bf16[16,8,32,256]{3,2,1,0:T(8,128)(2,1)} %get-tuple-element.141), channel_id=1, source_target_pairs={{0,1},{1,0},{2,3},{3,2},{4,5},{5,4},{6,7},{7,6},{8,9},{9,8},{10,11... | collective-permute-start | bytes 6291464 | tf_op jit(solution)/shard_map/ppermute | solution.py:654
  183.3 44.4 %collective-permute-start.43 = (bf16[16,5,32,256]{3,2,1,0:T(8,128)(2,1)}, bf16[16,5,32,256]{3,2,1,0:T(8,128)(2,1)S(1)}, u32[]{:S(2)}, u32[]{:S(2)}) collective-permute-start(bf16[16,5,32,256]{3,2,1,0:T(8,128)(2,1)} %get-tuple-element.131), channel_id=1, source_target_pairs={{0,1},{1,0},{2,3},{3,2},{4,5},{5,4},{6,7},{7,6},{8,9},{9,8},{10,11... | collective-permute-start | bytes 3932168 | tf_op jit(solution)/shard_map/ppermute | solution.py:654
  183.8 28.3 %collective-permute-start.33 = (bf16[1024,256]{1,0:T(8,128)(2,1)}, bf16[1024,256]{1,0:T(8,128)(2,1)}, u32[]{:S(2)}, u32[]{:S(2)}) collective-permute-start(bf16[1024,256]{1,0:T(8,128)(2,1)} %get-tuple-element.93), channel_id=1, source_target_pairs={{0,1},{1,0},{2,3},{3,2},{4,5},{5,4},{6,7},{7,6},{8,9},{9,8},{10,11... | collective-permute-start | bytes 1572872 | tf_op jit(solution)/shard_map/ppermute | solution.py:654
  202.6 17.2 %collective-permute-start.36 = (bf16[16,4,32,256]{3,2,1,0:T(8,128)(2,1)}, bf16[16,4,32,256]{3,2,1,0:T(8,128)(2,1)}, u32[]{:S(2)}, u32[]{:S(2)}) collective-permute-start(bf16[16,4,32,256]{3,2,1,0:T(8,128)(2,1)} %get-tuple-element.121), channel_id=1, source_target_pairs={{0,1},{1,0},{2,3},{3,2},{4,5},{5,4},{6,7},{7,6},{8,9},{9,8},{10,11... | collective-permute-start | bytes 3145736 | tf_op jit(solution)/shard_map/ppermute | solution.py:654
  211.9 15.7 %collective-permute-start.35 = (bf16[1024,256]{1,0:T(8,128)(2,1)}, bf16[1024,256]{1,0:T(8,128)(2,1)}, u32[]{:S(2)}, u32[]{:S(2)}) collective-permute-start(bf16[1024,256]{1,0:T(8,128)(2,1)} %get-tuple-element.119), channel_id=1, source_target_pairs={{0,1},{1,0},{2,3},{3,2},{4,5},{5,4},{6,7},{7,6},{8,9},{9,8},{10,11... | collective-permute-start | bytes 1572872 | tf_op jit(solution)/shard_map/ppermute | solution.py:654
  214.2 164.8 %all-to-all-start.1 = ((bf16[16,128,256]{2,1,0:T(8,128)(2,1)}), bf16[16,128,256]{2,1,0:T(8,128)(2,1)}, u32[]{:S(2)}, u32[]{:S(2)}) async-start(bf16[16,128,256]{2,1,0:T(8,128)(2,1)} %bitcast.50), calls=%async_computation.1 | async-start | bytes 2097152 | tf_op jit(solution)/shard_map/all_to_all | solution.py:751
  227.6 21.8 %collective-permute-start.39 = (bf16[4,4,32,256]{3,2,1,0:T(8,128)(2,1)}, bf16[4,4,32,256]{3,2,1,0:T(8,128)(2,1)S(1)}, u32[]{:S(2)}, u32[]{:S(2)}) collective-permute-start(bf16[4,4,32,256]{3,2,1,0:T(8,128)(2,1)} %get-tuple-element.125), channel_id=1, source_target_pairs={{0,6},{2,4},{4,2},{6,0},{8,14},{10,12},{12,10},{14,8},{16,22},{18,... | collective-permute-start | bytes 786440 | tf_op jit(solution)/shard_map/ppermute | solution.py:658
  227.8 24.7 %collective-permute-start.34 = (bf16[1024,256]{1,0:T(8,128)(2,1)S(1)}, bf16[1024,256]{1,0:T(8,128)(2,1)}, u32[]{:S(2)}, u32[]{:S(2)}) collective-permute-start(bf16[1024,256]{1,0:T(8,128)(2,1)S(1)} %copy-done.39), channel_id=1, source_target_pairs={{0,1},{1,0},{2,3},{3,2},{4,5},{5,4},{6,7},{7,6},{8,9},{9,8},{10,11... | collective-permute-start | bytes 1572872 | tf_op jit(solution)/shard_map/ppermute | solution.py:654
  239.2 15.4 %collective-permute-start.44 = (bf16[4,5,32,256]{3,2,1,0:T(8,128)(2,1)}, bf16[4,5,32,256]{3,2,1,0:T(8,128)(2,1)S(1)}, u32[]{:S(2)}, u32[]{:S(2)}) collective-permute-start(bf16[4,5,32,256]{3,2,1,0:T(8,128)(2,1)} %get-tuple-element.133), channel_id=1, source_target_pairs={{0,2},{2,0},{4,6},{6,4},{8,10},{10,8},{12,14},{14,12},{16,18},{18,... | collective-permute-start | bytes 983048 | tf_op jit(solution)/shard_map/ppermute | solution.py:658
  241.4 16.1 %collective-permute-start.45 = (bf16[4,5,32,256]{3,2,1,0:T(8,128)(2,1)}, bf16[4,5,32,256]{3,2,1,0:T(8,128)(2,1)S(1)}, u32[]{:S(2)}, u32[]{:S(2)}) collective-permute-start(bf16[4,5,32,256]{3,2,1,0:T(8,128)(2,1)} %get-tuple-element.134), channel_id=1, source_target_pairs={{0,4},{2,6},{4,0},{6,2},{8,12},{10,14},{12,8},{14,10},{16,20},{18,... | collective-permute-start | bytes 983048 | tf_op jit(solution)/shard_map/ppermute | solution.py:658
  249.4 82.8 %collective-permute-start.46 = (bf16[4,5,32,256]{3,2,1,0:T(8,128)(2,1)}, bf16[4,5,32,256]{3,2,1,0:T(8,128)(2,1)S(1)}, u32[]{:S(2)}, u32[]{:S(2)}) collective-permute-start(bf16[4,5,32,256]{3,2,1,0:T(8,128)(2,1)} %get-tuple-element.135), channel_id=1, source_target_pairs={{0,6},{2,4},{4,2},{6,0},{8,14},{10,12},{12,10},{14,8},{16,22},{18,... | collective-permute-start | bytes 983048 | tf_op jit(solution)/shard_map/ppermute | solution.py:658
  252.4 82.6 %collective-permute-start.40 = (bf16[4,32,256]{2,1,0:T(8,128)(2,1)}, bf16[4,32,256]{2,1,0:T(8,128)(2,1)S(1)}, u32[]{:S(2)}, u32[]{:S(2)}) collective-permute-start(bf16[4,32,256]{2,1,0:T(8,128)(2,1)} %get-tuple-element.127), channel_id=1, source_target_pairs={{0,8},{2,10},{4,12},{6,14},{8,0},{10,2},{12,4},{14,6},{16,24},{18,... | collective-permute-start | bytes 196616 | tf_op jit(solution)/shard_map/ppermute | solution.py:658
  254.7 80.9 %collective-permute-start.41 = (bf16[4,32,256]{2,1,0:T(8,128)(2,1)}, bf16[4,32,256]{2,1,0:T(8,128)(2,1)S(1)}, u32[]{:S(2)}, u32[]{:S(2)}) collective-permute-start(bf16[4,32,256]{2,1,0:T(8,128)(2,1)} %get-tuple-element.128), channel_id=1, source_target_pairs={{0,16},{2,18},{4,20},{6,22},{8,24},{10,26},{12,28},{14,30},{16,0},... | collective-permute-start | bytes 196616 | tf_op jit(solution)/shard_map/ppermute | solution.py:658
  257.5 81.9 %collective-permute-start.42 = (bf16[4,32,256]{2,1,0:T(8,128)(2,1)}, bf16[4,32,256]{2,1,0:T(8,128)(2,1)S(1)}, u32[]{:S(2)}, u32[]{:S(2)}) collective-permute-start(bf16[4,32,256]{2,1,0:T(8,128)(2,1)} %get-tuple-element.129), channel_id=1, source_target_pairs={{0,24},{2,26},{4,28},{6,30},{8,16},{10,18},{12,20},{14,22},{16,8},... | collective-permute-start | bytes 196616 | tf_op jit(solution)/shard_map/ppermute | solution.py:658
  347.9 22.8 %collective-permute-start.53 = (bf16[4,8,32,256]{3,2,1,0:T(8,128)(2,1)}, bf16[4,8,32,256]{3,2,1,0:T(8,128)(2,1)S(1)}, u32[]{:S(2)}, u32[]{:S(2)}) collective-permute-start(bf16[4,8,32,256]{3,2,1,0:T(8,128)(2,1)} %get-tuple-element.145), channel_id=1, source_target_pairs={{0,6},{2,4},{4,2},{6,0},{8,14},{10,12},{12,10},{14,8},{16,22},{18,... | collective-permute-start | bytes 1572872 | tf_op jit(solution)/shard_map/ppermute | solution.py:658
  (82 other events, 1476.0 us)
